TPU v7x, 1024 devices: a whole 4x8x16 slice. The times are simulated.
1024 devices in a mesh: ctx: 64 (over y, z_lo, core), ch: 16 (over x, z_hi).
Axes of the slice: x: 4, y: 8, z: 16 (z_hi: 4, z_lo: 4; z = z_hi * 4 + z_lo), core: 2. Of those that a mesh axis runs over, the one named last changes fastest.
Arguments:
- gate_input: bfloat16 [1024, 8192], P('ch', 'ctx'), may hold values from -6 to 6
- key_input: bfloat16 [1024, 8192], P('ch', 'ctx'), may hold values from -6 to 6
- value_input: bfloat16 [1024, 8192], P('ch', 'ctx'), may hold values from -6 to 6
- features: float32 [64, 8192], P('ch', 'ctx'), may hold values from -6 to 6
- filter_weight: float32 [64, 1024], P(None, 'ch'), may hold values from -0.75 to 0.75
- out_grad: bfloat16 [1024, 8192], P('ch', 'ctx'), may hold values from -6 to 6
Outputs:
- output: bfloat16 [1024, 8192], P('ch', 'ctx')
- gate_grad: bfloat16 [1024, 8192], P('ch', 'ctx')
- key_grad: bfloat16 [1024, 8192], P('ch', 'ctx')
- value_grad: bfloat16 [1024, 8192], P('ch', 'ctx')
- weight_grad: float32 [64, 1024], P(None, 'ch')
All inputs are finite; a program needn't handle non-finite values.
Results may differ from a plain program's by a relative error of at most 0.0019.
Values sent between devices are 32-bit elements; how exact they have to be, the bound alone decides.
A program may use at most 32 MiB of HBM per device.

v0:
```python
import math

import jax
import jax.numpy as jnp
from jax import lax
from jax.sharding import PartitionSpec as P

highest = lax.Precision.HIGHEST


def cos_sin(row_index, col_index, period):
    phases = row_index[:, None] * col_index[None, :] % period
    angles = phases.astype(jnp.float32) * (2.0 * math.pi / period)
    return (jnp.cos(angles), jnp.sin(angles))


def split_length(length):
    chosen = 1
    for factor in range(1, math.isqrt(length) + 1):
        if length % factor == 0:
            chosen = factor
    return chosen


def local_dft(real, imag, orient):
    groups, length, span_cols = real.shape
    outer_len = split_length(length)
    inner_len = length // outer_len
    outer_index = jnp.arange(outer_len, dtype=jnp.int32)
    inner_index = jnp.arange(inner_len, dtype=jnp.int32)
    small_cos, small_sin = cos_sin(outer_index, outer_index, outer_len)
    turn_cos, turn_sin = cos_sin(outer_index, inner_index, length)
    large_cos, large_sin = cos_sin(inner_index, inner_index, inner_len)
    real_view = real.reshape(groups, outer_len, inner_len, span_cols)
    imag_view = imag.reshape(groups, outer_len, inner_len, span_cols)
    section_real = jnp.einsum(
        "kn,jnqw->jkqw", small_cos, real_view, precision=highest
    ) - orient * jnp.einsum("kn,jnqw->jkqw", small_sin, imag_view, precision=highest)
    section_imag = jnp.einsum(
        "kn,jnqw->jkqw", small_cos, imag_view, precision=highest
    ) + orient * jnp.einsum("kn,jnqw->jkqw", small_sin, real_view, precision=highest)
    turn_cos = turn_cos[None, :, :, None]
    turn_sin = turn_sin[None, :, :, None]
    turned_real = section_real * turn_cos - orient * section_imag * turn_sin
    turned_imag = section_imag * turn_cos + orient * section_real * turn_sin
    final_real = jnp.einsum(
        "mq,jkqw->jmkw", large_cos, turned_real, precision=highest
    ) - orient * jnp.einsum("mq,jkqw->jmkw", large_sin, turned_imag, precision=highest)
    final_imag = jnp.einsum(
        "mq,jkqw->jmkw", large_cos, turned_imag, precision=highest
    ) + orient * jnp.einsum("mq,jkqw->jmkw", large_sin, turned_real, precision=highest)
    return (
        final_real.reshape(groups, length, span_cols),
        final_imag.reshape(groups, length, span_cols),
    )


def plan_tables(length):
    shards = lax.axis_size("ctx")
    my_index = lax.axis_index("ctx")
    stride = length // shards
    doubled = 2 * shards
    padded = doubled * length
    outer_rows = jnp.arange(doubled, dtype=jnp.int32)
    block_cos, block_sin = cos_sin(outer_rows, jnp.arange(shards, dtype=jnp.int32), doubled)
    local_cols = my_index * stride + jnp.arange(stride, dtype=jnp.int32)
    twist_cos, twist_sin = cos_sin(outer_rows, local_cols, padded)
    return (block_cos, block_sin, twist_cos[:, :, None], twist_sin[:, :, None], padded)


def to_spectrum(signal, tables):
    block_cos, block_sin, twist_cos, twist_sin, padded = tables
    length, columns = signal.shape
    spread = lax.all_to_all(
        signal.reshape(1, length, columns), "ctx", split_axis=1, concat_axis=0, tiled=True
    )
    real_outer = jnp.einsum("ka,abw->kbw", block_cos, spread, precision=highest)
    imag_outer = -jnp.einsum("ka,abw->kbw", block_sin, spread, precision=highest)
    real_twist = real_outer * twist_cos + imag_outer * twist_sin
    imag_twist = imag_outer * twist_cos - real_outer * twist_sin
    owned = lax.all_to_all(
        jnp.stack([real_twist, imag_twist]), "ctx", split_axis=1, concat_axis=2, tiled=True
    )
    return local_dft(owned[0], owned[1], -1.0)


def to_time(spec_real, spec_imag, tables):
    block_cos, block_sin, twist_cos, twist_sin, padded = tables
    back_real, back_imag = local_dft(spec_real, spec_imag, 1.0)
    returned = lax.all_to_all(
        jnp.stack([back_real, back_imag]), "ctx", split_axis=2, concat_axis=1, tiled=True
    )
    real_twist = returned[0] * twist_cos - returned[1] * twist_sin
    imag_twist = returned[1] * twist_cos + returned[0] * twist_sin
    in_time = (
        jnp.einsum("ka,kbw->abw", block_cos, real_twist, precision=highest)
        - jnp.einsum("ka,kbw->abw", block_sin, imag_twist, precision=highest)
    ) * (1.0 / padded)
    placed = lax.all_to_all(in_time, "ctx", split_axis=0, concat_axis=1, tiled=True)
    return placed.reshape(placed.shape[1], placed.shape[2])


def on_device(gate_input, key_input, value_input, features, filter_weight, out_grad):
    channels, length = gate_input.shape
    shards = lax.axis_size("ctx")
    seq_len = length * shards
    scaling = 1.0 / math.sqrt(seq_len)
    gate_vals = gate_input.astype(jnp.float32).T
    key_vals = key_input.astype(jnp.float32).T
    value_vals = value_input.astype(jnp.float32).T
    upstream = out_grad.astype(jnp.float32).T
    mixed_in = key_vals * value_vals
    inner_term = upstream * gate_vals
    feats_all = lax.all_gather(features, "ch", axis=0, tiled=True).T
    tables = plan_tables(length)
    second = jnp.dot(feats_all, filter_weight, precision=highest) * scaling
    second_width = second.shape[1]
    spec_real, spec_imag = to_spectrum(jnp.concatenate([mixed_in, second], axis=1), tables)
    mixed_real = spec_real[:, :, :channels]
    mixed_imag = spec_imag[:, :, :channels]
    other_real = spec_real[:, :, channels : channels + second_width]
    other_imag = spec_imag[:, :, channels : channels + second_width]
    conv_real = mixed_real * other_real - mixed_imag * other_imag
    conv_imag = mixed_real * other_imag + mixed_imag * other_real
    conv_out = to_time(conv_real, conv_imag, tables)
    inner_real, inner_imag = to_spectrum(inner_term, tables)
    back_real = inner_real * other_real + inner_imag * other_imag
    back_imag = inner_imag * other_real - inner_real * other_imag
    taps_real = inner_real * mixed_real + inner_imag * mixed_imag
    taps_imag = inner_imag * mixed_real - inner_real * mixed_imag
    both_time = to_time(
        jnp.concatenate([back_real, taps_real], axis=2),
        jnp.concatenate([back_imag, taps_imag], axis=2),
        tables,
    )
    mixed_grad = both_time[:, :channels]
    taps_grad = both_time[:, channels:]
    partial_grad = jnp.einsum("tf,tc->fc", feats_all, taps_grad, precision=highest) * (
        scaling * scaling
    )
    output = (gate_vals * conv_out).T.astype(jnp.bfloat16)
    gate_grad = (upstream * conv_out).T.astype(jnp.bfloat16)
    weight_grad = lax.psum(partial_grad, "ctx")
    key_grad = (mixed_grad * value_vals).T.astype(jnp.bfloat16)
    value_grad = (mixed_grad * key_vals).T.astype(jnp.bfloat16)
    return (output, gate_grad, key_grad, value_grad, weight_grad)


def solution(mesh):
    placed = (
        P("ch", "ctx"),
        P("ch", "ctx"),
        P("ch", "ctx"),
        P("ch", "ctx"),
        P(None, "ch"),
        P("ch", "ctx"),
    )
    return jax.shard_map(
        on_device,
        mesh=mesh,
        in_specs=placed,
        out_specs=(P("ch", "ctx"), P("ch", "ctx"), P("ch", "ctx"), P("ch", "ctx"), P(None, "ch")),
        check_vma=False,
    )
```

profile of v0, /device:TPU:1, one launch (start us, length us, event | category | flops | bytes accessed | tf_op | source)
XLA Modules:
  0.0 468.9 jit_solution(3528508845379581548)
XLA Ops:
  2.0 0.8 reduce
  3.5 18.2 %all-to-all-start.4 = ((f32[64,1,128]{2,1,0:T(1,128)}), f32[64,1,128]{2,1,0:T(1,128)S(1)}, u32[]{:S(2)}, u32[]{:S(2)}) async-start(f32[64,1,128]{2,1,0:T(1,128)} %reshape.197), calls=%async_computation.4 | async-start | bytes 65536 | tf_op jit(solution)/shard_map/all_to_all | solution.py:74
  22.4 50.2 %all-gather = f32[16,4,128]{2,1,0:T(4,128)S(1)} all-gather(f32[1,4,128]{2,1,0:T(4,128)S(1)} %bitcast.327), channel_id=1, replica_groups=mesh['ctx'=64,'ch'=16] {'ch'}, dimensions={0}, use_global_device_ids=true | all-gather | bytes 34816 | tf_op jit(solution)/shard_map/all_gather | solution.py:114
  74.2 17.9 %all-to-all-start = ((f32[1,128,128]{2,0,1:T(1,128)}), f32[1,128,128]{2,0,1:T(1,128)S(1)}, u32[]{:S(2)}, u32[]{:S(2)}) async-start(f32[1,128,128]{2,0,1:T(1,128)} %copy.168), calls=%async_computation | async-start | bytes 131072 | tf_op jit(solution)/shard_map/all_to_all | solution.py:74
  94.0 0.9 reshape.199
  94.9 7.3 %all-to-all-done = f32[1,128,128]{2,0,1:T(1,128)S(1)} async-done(((f32[1,128,128]{2,0,1:T(1,128)}), f32[1,128,128]{2,0,1:T(1,128)S(1)}, u32[]{:S(2)}, u32[]{:S(2)}) %all-to-all-start) | async-done | bytes 65568 | tf_op jit(solution)/shard_map/all_to_all | solution.py:74
  102.1 4.4 all-to-all-start.5
  107.6 0.9 copy.171
  108.5 9.1 %all-to-all-done.5 = f32[64,1,512]{2,1,0:T(1,128)S(1)} async-done(((f32[64,1,512]{2,1,0:T(1,128)}), f32[64,1,512]{2,1,0:T(1,128)S(1)}, u32[]{:S(2)}, u32[]{:S(2)}) %all-to-all-start.5) | async-done | bytes 131104 | tf_op jit(solution)/shard_map/all_to_all | solution.py:81
  117.5 4.5 all-to-all-start.1
  122.0 1.0 reduce.2
  126.0 9.6 %all-to-all-done.1 = f32[2,128,2,128]{3,2,0,1:T(2,128)S(1)} async-done(((f32[2,128,2,128]{3,2,0,1:T(2,128)}), f32[2,128,2,128]{3,2,0,1:T(2,128)S(1)}, u32[]{:S(2)}, u32[]{:S(2)}) %all-to-all-start.1) | async-done | bytes 262176 | tf_op jit(solution)/shard_map/all_to_all | solution.py:81
  143.7 0.9 reshape.193
  144.6 4.5 all-to-all-start.2
  149.9 0.9 copy.231
  150.8 9.3 %all-to-all-done.2 = f32[64,1,512]{2,1,0:T(1,128)S(1)} async-done(((f32[64,1,512]{2,1,0:T(1,128)}), f32[64,1,512]{2,1,0:T(1,128)S(1)}, u32[]{:S(2)}, u32[]{:S(2)}) %all-to-all-start.2) | async-done | bytes 131104 | tf_op jit(solution)/shard_map/all_to_all | solution.py:90
  160.1 4.5 all-to-all-start.6
  164.6 1.0 reduce.3
  167.7 10.5 %all-to-all-done.6 = f32[2,2,128,128]{3,1,0,2:T(2,128)S(1)} async-done(((f32[2,2,128,128]{3,1,0,2:T(2,128)}), f32[2,2,128,128]{3,1,0,2:T(2,128)S(1)}, u32[]{:S(2)}, u32[]{:S(2)}) %all-to-all-start.6) | async-done | bytes 262176 | tf_op jit(solution)/shard_map/all_to_all | solution.py:90
  178.2 4.5 all-to-all-start.3
  184.5 7.9 %all-to-all-done.3 = f32[64,1,128]{2,1,0:T(1,128)S(1)} async-done(((f32[64,1,128]{2,1,0:T(1,128)}), f32[64,1,128]{2,1,0:T(1,128)S(1)}, u32[]{:S(2)}, u32[]{:S(2)}) %all-to-all-start.3) | async-done | bytes 32800 | tf_op jit(solution)/shard_map/all_to_all | solution.py:99
  192.4 4.7 %all-to-all-start.7 = ((f32[64,2,128]{2,1,0:T(2,128)}), f32[64,2,128]{2,1,0:T(2,128)S(1)}, u32[]{:S(2)}, u32[]{:S(2)}) async-start(f32[64,2,128]{2,1,0:T(2,128)} %copy.235), calls=%async_computation.7 | async-start | bytes 131072 | tf_op jit(solution)/shard_map/all_to_all | solution.py:99
  199.3 8.0 %all-to-all-done.7 = f32[64,2,128]{2,1,0:T(2,128)S(1)} async-done(((f32[64,2,128]{2,1,0:T(2,128)}), f32[64,2,128]{2,1,0:T(2,128)S(1)}, u32[]{:S(2)}, u32[]{:S(2)}) %all-to-all-start.7) | async-done | bytes 65568 | tf_op jit(solution)/shard_map/all_to_all | solution.py:99
  207.6 259.9 %psum.7 = f32[64,64]{0,1:T(8,128)S(1)} all-reduce(f32[64,64]{0,1:T(8,128)S(1)} %fusion.18), channel_id=1, replica_groups=mesh['ctx'=64,'ch'=16] {'ctx'}, use_global_device_ids=true, to_apply=%region_0.1 | all-reduce | flops 4096 | bytes 32768 | tf_op jit(solution)/shard_map/psum | solution.py:143
  (113 shorter events, 26.2 us)
Async XLA Ops:
  0.6 72.0 %copy-start = (f32[64,64]{1,0:T(8,128)S(1)}, f32[64,64]{1,0:T(8,128)}, u32[]{:S(2)}) copy-start(f32[64,64]{1,0:T(8,128)} %param.10) | copy-start | bytes 49156
  3.5 70.7 %all-to-all-start.4 = ((f32[64,1,128]{2,1,0:T(1,128)}), f32[64,1,128]{2,1,0:T(1,128)S(1)}, u32[]{:S(2)}, u32[]{:S(2)}) async-start(f32[64,1,128]{2,1,0:T(1,128)} %reshape.197), calls=%async_computation.4 | async-start | bytes 65536 | tf_op jit(solution)/shard_map/all_to_all | solution.py:74
  21.7 0.7 copy-start.5
  72.7 0.7 copy-start.3
  72.7 0.7 copy-start.4
  74.2 27.9 %all-to-all-start = ((f32[1,128,128]{2,0,1:T(1,128)}), f32[1,128,128]{2,0,1:T(1,128)S(1)}, u32[]{:S(2)}, u32[]{:S(2)}) async-start(f32[1,128,128]{2,0,1:T(1,128)} %copy.168), calls=%async_computation | async-start | bytes 131072 | tf_op jit(solution)/shard_map/all_to_all | solution.py:74
  102.1 15.4 %all-to-all-start.5 = ((f32[64,1,512]{2,1,0:T(1,128)}), f32[64,1,512]{2,1,0:T(1,128)S(1)}, u32[]{:S(2)}, u32[]{:S(2)}) async-start(f32[64,1,512]{2,1,0:T(1,128)} %reshape.199), calls=%async_computation.5 | async-start | bytes 262144 | tf_op jit(solution)/shard_map/all_to_all | solution.py:81
  117.5 18.1 %all-to-all-start.1 = ((f32[2,128,2,128]{3,2,0,1:T(2,128)}), f32[2,128,2,128]{3,2,0,1:T(2,128)S(1)}, u32[]{:S(2)}, u32[]{:S(2)}) async-start(f32[2,128,2,128]{3,2,0,1:T(2,128)} %copy.171), calls=%async_computation.1 | async-start | bytes 524288 | tf_op jit(solution)/shard_map/all_to_all | solution.py:81
  144.6 15.5 %all-to-all-start.2 = ((f32[64,1,512]{2,1,0:T(1,128)}), f32[64,1,512]{2,1,0:T(1,128)S(1)}, u32[]{:S(2)}, u32[]{:S(2)}) async-start(f32[64,1,512]{2,1,0:T(1,128)} %reshape.193), calls=%async_computation.2 | async-start | bytes 262144 | tf_op jit(solution)/shard_map/all_to_all | solution.py:90
  160.1 18.1 %all-to-all-start.6 = ((f32[2,2,128,128]{3,1,0,2:T(2,128)}), f32[2,2,128,128]{3,1,0,2:T(2,128)S(1)}, u32[]{:S(2)}, u32[]{:S(2)}) async-start(f32[2,2,128,128]{3,1,0,2:T(2,128)} %copy.231), calls=%async_computation.6 | async-start | bytes 524288 | tf_op jit(solution)/shard_map/all_to_all | solution.py:90
  178.2 14.2 %all-to-all-start.3 = ((f32[64,1,128]{2,1,0:T(1,128)}), f32[64,1,128]{2,1,0:T(1,128)S(1)}, u32[]{:S(2)}, u32[]{:S(2)}) async-start(f32[64,1,128]{2,1,0:T(1,128)} %reshape.195), calls=%async_computation.3 | async-start | bytes 65536 | tf_op jit(solution)/shard_map/all_to_all | solution.py:99
  192.4 14.9 %all-to-all-start.7 = ((f32[64,2,128]{2,1,0:T(2,128)}), f32[64,2,128]{2,1,0:T(2,128)S(1)}, u32[]{:S(2)}, u32[]{:S(2)}) async-start(f32[64,2,128]{2,1,0:T(2,128)} %copy.235), calls=%async_computation.7 | async-start | bytes 131072 | tf_op jit(solution)/shard_map/all_to_all | solution.py:99
  197.9 0.7 copy-start.1
  197.9 0.7 copy-start.2
where the time goes:
time: 472 us; the launch traced here: 469 us
  blocking collectives  310 us (66%)
  starting transfers between devices  63.2 us (13%)
  waiting for transfers between devices  61.6 us (13%)
  matrix products  13.7 us (3%)
  local copies, waits for them, and re-layouts  12 us (3%)
  other arithmetic  6.92 us (1%)
    psum x1, blocking collectives, on_device(): weight_grad = lax.psum(partial_grad, 'ctx')  260 us
    all_gather x1, blocking collectives, on_device(): feats_all = lax.all_gather(features, 'ch', axis=0, tiled=True).T  50.2 us
    all_to_all x2, starting transfers between devices, to_spectrum(): lax.all_to_all(signal.reshape(1, length, columns), 'ctx', split_axis=1, c...  36.1 us
    all_to_all x2, waiting for transfers between devices, to_time(): lax.all_to_all(jnp.stack([back_real, back_imag]), 'ctx', split_axis=2, co...  19.8 us
    all_to_all x2, waiting for transfers between devices, to_spectrum(): lax.all_to_all(jnp.stack([real_twist, imag_twist]), 'ctx', split_axis=1,...  18.7 us
    all_to_all x2, waiting for transfers between devices, to_time(): lax.all_to_all(in_time, 'ctx', split_axis=0, concat_axis=1, tiled=True)  15.9 us
  transfers between devices with their start and end apart: 8, of which 7 were waited for; matrix products, arithmetic and copies ran while one was open for 4% of the time, Pallas kernels for 0%

commit v1 on v0

v1 whole, which is shorter than its diff:
```python
import functools
import math

import jax
import jax.numpy as jnp
import numpy as np
from jax import lax
from jax.experimental import pallas as pl
from jax.experimental.pallas import tpu as pltpu
from jax.sharding import PartitionSpec as P

MESH = pl.DeviceIdType.MESH
HIGHEST = lax.Precision.HIGHEST
f32 = jnp.float32
bf16 = jnp.bfloat16
LANES = 128


def make_tables(shards):
    outer = 2 * shards
    padded = outer * LANES
    rows = -(-(shards + 1) // 8) * 8
    r = np.arange(rows)
    live = (r <= shards).astype(np.float64)
    natural = np.arange(shards)
    by_parity = np.concatenate([natural[0::2], natural[1::2]])

    def angles(left, right, period):
        return 2.0 * np.pi * ((left[:, None] * right[None, :]) % period) / period

    first, last = [], []
    weight = np.where((r == 0) | (r == shards), 1.0, 2.0) * live / padded
    for order in (natural, by_parity):
        turn = angles(r, order, outer)
        table = np.concatenate([np.cos(turn), np.sin(turn)], axis=0) * np.tile(live, 2)[:, None]
        first.append(table)
        turn = angles(order, r, outer)
        table = np.concatenate([np.cos(turn) * weight, -np.sin(turn) * weight], axis=1)
        last.append(table)
    q = np.arange(LANES)
    turn = angles(q, q, LANES)
    cos, sin = np.cos(turn), np.sin(turn)
    forward = np.block([[cos, -sin], [sin, cos]])
    backward = np.block([[cos, sin], [-sin, cos]])
    turn = angles(r, q, padded)
    twist = [np.cos(turn), np.sin(turn)]
    return tuple(np.stack(table).astype(np.float32) for table in (first, last, [forward, backward], twist))


def halves(x):
    high = x.astype(bf16)
    return high, (x - high.astype(f32)).astype(bf16)


def dot(a, b):
    return jnp.dot(a, b, preferred_element_type=f32)


def dot_t(a, b):
    return lax.dot_general(a, b, (((1,), (1,)), ((), ())), precision=HIGHEST, preferred_element_type=f32)


def spectra(signals, first, mid, cos, sin):
    rows = cos.shape[0]
    high, low = halves(jnp.concatenate(signals, axis=1))
    outer = dot(first, jnp.concatenate([high, low, high], axis=0))
    turned = []
    for index in range(len(signals)):
        part = outer[:, index * LANES : (index + 1) * LANES]
        along, across = part[:rows], part[rows:]
        turned.append(
            jnp.concatenate([along * cos - across * sin, -(across * cos + along * sin)], axis=1)
        )
    high, low = halves(jnp.concatenate(turned, axis=0))
    return dot(high, mid[0]) + dot(low, mid[0]) + dot(high, mid[1])


def signals_of(products, last, mid, cos, sin):
    rows = cos.shape[0]
    high, low = halves(jnp.concatenate(products, axis=0))
    inner = dot(high, mid[0]) + dot(low, mid[0]) + dot(high, mid[1])
    turned = []
    for index in range(len(products)):
        part = inner[index * rows : (index + 1) * rows]
        real, imag = part[:, :LANES], part[:, LANES:]
        turned.append(jnp.concatenate([real * cos - imag * sin, imag * cos + real * sin], axis=0))
    high, low = halves(jnp.concatenate(turned, axis=1))
    return dot(last[0], high) + dot(last[0], low) + dot(last[1], high)


def times(a, b):
    ar, ai, br, bi = a[:, :LANES], a[:, LANES:], b[:, :LANES], b[:, LANES:]
    return jnp.concatenate([ar * br - ai * bi, ar * bi + ai * br], axis=1)


def times_conj(a, b):
    ar, ai, br, bi = a[:, :LANES], a[:, LANES:], b[:, :LANES], b[:, LANES:]
    return jnp.concatenate([ar * br + ai * bi, ai * br - ar * bi], axis=1)


def kernel(
    shards,
    groups,
    gate_in,
    key_in,
    value_in,
    feats_in,
    weight_in,
    upstream_in,
    first_in,
    last_in,
    mid_in,
    twist_in,
    output,
    gate_grad,
    key_grad,
    value_grad,
    weight_grad,
    gate,
    key,
    value,
    upstream,
    weight,
    first,
    last,
    mid,
    twist,
    first_split,
    last_split,
    mid_split,
    feats,
    send_sig,
    recv_sig,
    send_filt,
    recv_filt,
    send_taps,
    recv_taps,
    send_part,
    recv_part,
    send_sum,
    recv_sum,
    send_out,
    recv_out,
    in_sems,
    table_sems,
    own_sem,
    send_sems,
    recv_sems,
):
    me = lax.axis_index("ctx")
    group = lax.axis_index("ch")
    owners = shards // 2
    chip = me // 2
    core = me % 2
    scaling = 1.0 / math.sqrt(shards * LANES)

    inputs = [
        pltpu.make_async_copy(src, dst, in_sems.at[n])
        for n, (src, dst) in enumerate(
            [(key_in, key), (value_in, value), (upstream_in, upstream), (gate_in, gate), (weight_in, weight)]
        )
    ]
    tables = [
        pltpu.make_async_copy(src, dst, table_sems.at[n])
        for n, (src, dst) in enumerate([(first_in, first), (mid_in, mid), (twist_in, twist), (last_in, last)])
    ]

    def push(src, dst, phase, where):
        pltpu.make_async_remote_copy(
            src_ref=src,
            dst_ref=dst,
            send_sem=send_sems.at[phase],
            recv_sem=recv_sems.at[phase],
            device_id=where,
            device_id_type=MESH,
        ).start()

    def loop(low, high, step):
        def body(k, carry):
            step(k)
            return carry

        lax.fori_loop(low, high, body, 0)

    def arrived(ref, count, phase):
        part = ref.at[pl.ds(0, count)]
        pltpu.make_async_copy(part, part, recv_sems.at[phase]).wait()

    def sent(ref, count, phase):
        part = ref.at[pl.ds(0, count)]
        pltpu.make_async_copy(part, part, send_sems.at[phase]).wait()

    for copy in inputs:
        copy.start()

    barrier = pltpu.get_barrier_semaphore()

    @pl.when(core == 1)
    def _():
        def tell(k):
            pl.semaphore_signal(barrier, inc=1, device_id={"ctx": me ^ k, "ch": group}, device_id_type=MESH)

        def tell_groups(k):
            other = group ^ k
            pl.semaphore_signal(barrier, inc=1, device_id={"ctx": me, "ch": other}, device_id_type=MESH)
            pl.semaphore_signal(barrier, inc=1, device_id={"ctx": me - 1, "ch": other}, device_id_type=MESH)

        loop(1, groups, tell_groups)
        loop(1, shards, tell)
        for copy in tables:
            copy.start()
        pl.semaphore_wait(barrier, owners - 1 + groups - 1)

    @pl.when(core == 0)
    def _():
        pl.semaphore_wait(barrier, owners + groups - 1)

    def push_feats(k):
        push(feats_in, feats.at[core * groups + group], 0, {"ctx": 2 * chip + 1, "ch": group ^ k})

    loop(1, groups, push_feats)
    own_feats = pltpu.make_async_copy(feats_in, feats.at[core * groups + group], own_sem)

    @pl.when(core == 0)
    def _():
        push_feats(0)

    @pl.when(core == 1)
    def _():
        own_feats.start()

    for copy in inputs[:4]:
        copy.wait()
    key_vals, value_vals = key[...].astype(f32), value[...].astype(f32)
    gate_vals, up_vals = gate[...].astype(f32), upstream[...].astype(f32)
    mixed, inner = key_vals * value_vals, up_vals * gate_vals
    send_sig[:, 0, :] = mixed[:owners]
    send_sig[:, 1, :] = mixed[owners:]
    send_sig[:, 2, :] = inner[:owners]
    send_sig[:, 3, :] = inner[owners:]

    def push_sig(k):
        to = chip ^ k
        push(send_sig.at[to], recv_sig.at[me], 1, {"ctx": 2 * to + 1, "ch": group})

    loop(1, owners, push_sig)

    @pl.when(core == 0)
    def _():
        push_sig(0)

    inputs[4].wait()

    @pl.when(core == 1)
    def _():
        recv_sig[pl.ds(me, 1)] = send_sig[pl.ds(chip, 1)]
        eye = (
            lax.broadcasted_iota(jnp.int32, (2 * owners, 2 * owners), 0)
            == lax.broadcasted_iota(jnp.int32, (2 * owners, 2 * owners), 1)
        ).astype(f32)
        weight_t = dot_t(eye, weight[...])
        for copy in tables:
            copy.wait()
        cos, sin = twist[0], twist[1]
        rows = cos.shape[0]
        for n in range(2):
            high, low = halves(first[n])
            first_split[n] = jnp.concatenate([high, high, low], axis=1)
            last_split[2 * n], last_split[2 * n + 1] = halves(last[n])
            mid_split[2 * n], mid_split[2 * n + 1] = halves(mid[n])
        forward, backward = (mid_split[0], mid_split[1]), (mid_split[2], mid_split[3])
        lasts = [(last_split[0], last_split[1]), (last_split[2], last_split[3])]

        own_feats.wait()
        arrived(feats, 2 * groups - 1, 0)
        per = feats.shape[1]
        feats_all = jnp.concatenate(
            [
                feats[:groups].reshape(groups * per, LANES),
                feats[groups:].reshape(groups * per, LANES),
            ],
            axis=1,
        )
        filt = jnp.dot(weight_t, feats_all, precision=HIGHEST, preferred_element_type=f32) * scaling
        send_filt[:, 0, :] = filt[:owners, :LANES]
        send_filt[:, 1, :] = filt[:owners, LANES:]
        send_filt[:, 2, :] = filt[owners:, :LANES]
        send_filt[:, 3, :] = filt[owners:, LANES:]

        def push_filt(k):
            to = chip ^ k
            push(send_filt.at[to], recv_filt.at[chip], 2, {"ctx": 2 * to + 1, "ch": group})

        loop(1, owners, push_filt)
        recv_filt[pl.ds(chip, 1)] = send_filt[pl.ds(chip, 1)]

        arrived(recv_sig, shards - 1, 1)
        specs = spectra([recv_sig[:, n, :] for n in range(4)], first_split[0], forward, cos, sin)
        mixed_specs = [specs[:rows], specs[rows : 2 * rows]]
        inner_specs = [specs[2 * rows : 3 * rows], specs[3 * rows :]]
        taps = signals_of(
            [times_conj(inner_specs[n], mixed_specs[n]) for n in range(2)], lasts[1], backward, cos, sin
        )
        send_taps[:, 0, :] = taps[:owners, :LANES]
        send_taps[:, 1, :] = taps[owners:, :LANES]
        send_taps[:, 2, :] = taps[:owners, LANES:]
        send_taps[:, 3, :] = taps[owners:, LANES:]

        def push_taps(k):
            to = chip ^ k
            push(send_taps.at[to], recv_taps.at[chip], 3, {"ctx": 2 * to + 1, "ch": group})

        loop(1, owners, push_taps)
        recv_taps[pl.ds(chip, 1)] = send_taps[pl.ds(chip, 1)]

        arrived(recv_filt, owners - 1, 2)
        filt_specs = spectra(
            [
                jnp.concatenate([recv_filt[:, 2 * n, :], recv_filt[:, 2 * n + 1, :]], axis=0)
                for n in range(2)
            ],
            first_split[1],
            forward,
            cos,
            sin,
        )
        filt_specs = [filt_specs[:rows], filt_specs[rows:]]
        results = signals_of(
            [times(mixed_specs[n], filt_specs[n]) for n in range(2)]
            + [times_conj(inner_specs[n], filt_specs[n]) for n in range(2)],
            lasts[0],
            backward,
            cos,
            sin,
        )
        for n in range(4):
            send_out[:, n, :] = results[:, n * LANES : (n + 1) * LANES]

        def push_out(k):
            to = me ^ k
            push(send_out.at[to], recv_out.at[chip], 4, {"ctx": to, "ch": group})

        loop(1, shards, push_out)
        recv_out[pl.ds(chip, 1)] = send_out[pl.ds(me, 1)]

        arrived(recv_taps, owners - 1, 3)
        taps_here = jnp.concatenate(
            [
                jnp.concatenate([recv_taps[:, 0, :], recv_taps[:, 1, :]], axis=1),
                jnp.concatenate([recv_taps[:, 2, :], recv_taps[:, 3, :]], axis=1),
            ],
            axis=0,
        )
        part = dot_t(taps_here, feats_all)
        send_part[:, 0, :] = jnp.concatenate([part[:owners], part[owners:]], axis=1)

        def push_part(k):
            to = chip ^ k
            push(send_part.at[to], recv_part.at[chip], 5, {"ctx": 2 * to + 1, "ch": group})

        loop(1, owners, push_part)
        recv_part[pl.ds(chip, 1)] = send_part[pl.ds(chip, 1)]

        arrived(recv_part, owners - 1, 5)
        send_sum[pl.ds(0, 1)] = jnp.sum(recv_part[...], axis=0, keepdims=True) * (scaling * scaling)

        def push_sum(k):
            push(send_sum.at[0], recv_sum.at[chip], 6, {"ctx": me ^ k, "ch": group})

        loop(1, shards, push_sum)
        recv_sum[pl.ds(chip, 1)] = send_sum[pl.ds(0, 1)]
        arrived(recv_out, owners - 1, 4)
        sent(send_filt, owners - 1, 2)
        sent(send_taps, owners - 1, 3)
        sent(send_out, shards - 1, 4)
        sent(send_part, owners - 1, 5)
        sent(feats, groups - 1, 0)
        sent(send_sig, owners - 1, 1)

    @pl.when(core == 0)
    def _():
        arrived(recv_out, owners, 4)
        sent(feats, groups, 0)
        sent(send_sig, owners, 1)

    conv = jnp.concatenate([recv_out[:, 0, :], recv_out[:, 1, :]], axis=0)
    mixed_grad = jnp.concatenate([recv_out[:, 2, :], recv_out[:, 3, :]], axis=0)
    output[...] = (gate[...].astype(f32) * conv).astype(bf16)
    gate_grad[...] = (upstream[...].astype(f32) * conv).astype(bf16)
    key_grad[...] = (mixed_grad * value[...].astype(f32)).astype(bf16)
    value_grad[...] = (mixed_grad * key[...].astype(f32)).astype(bf16)

    @pl.when(core == 1)
    def _():
        arrived(recv_sum, owners - 1, 6)
        sent(send_sum, shards - 1, 6)

    @pl.when(core == 0)
    def _():
        arrived(recv_sum, owners, 6)

    total = recv_sum[:, 0, :]
    half = total.shape[1] // 2
    grad_rows = jnp.concatenate([total[:, :half], total[:, half:]], axis=0)
    eye = (
        lax.broadcasted_iota(jnp.int32, (half, half), 0) == lax.broadcasted_iota(jnp.int32, (half, half), 1)
    ).astype(f32)
    weight_grad[...] = dot_t(eye, grad_rows)


def on_device(gate_input, key_input, value_input, features, filter_weight, out_grad):
    shards, groups = lax.axis_size("ctx"), lax.axis_size("ch")
    channels, length = gate_input.shape
    feat = filter_weight.shape[0]
    owners = shards // 2
    assert channels == 2 * owners and length == LANES and feat == LANES // 2
    tables = make_tables(shards)
    hbm = pl.BlockSpec(memory_space=pl.ANY)
    vmem = pl.BlockSpec(memory_space=pltpu.VMEM)
    rows = lambda count, width: pltpu.VMEM((count, width, LANES), f32)
    block = jax.ShapeDtypeStruct((channels, length), bf16)
    per = features.shape[0]
    return pl.pallas_call(
        functools.partial(kernel, shards, groups),
        out_shape=(block, block, block, block, jax.ShapeDtypeStruct((feat, channels), f32)),
        in_specs=[hbm] * 10,
        out_specs=(vmem,) * 5,
        scratch_shapes=[
            *[pltpu.VMEM((channels, length), bf16)] * 4,
            pltpu.VMEM(filter_weight.shape, f32),
            *[pltpu.VMEM(table.shape, f32) for table in tables],
            pltpu.VMEM((2, tables[0].shape[1], 3 * tables[0].shape[2]), bf16),
            pltpu.VMEM((4, *tables[1].shape[1:]), bf16),
            pltpu.VMEM((4, *tables[2].shape[1:]), bf16),
            rows(2 * groups, per),
            rows(owners, 4),
            rows(shards, 4),
            rows(owners, 4),
            rows(owners, 4),
            rows(owners, 4),
            rows(owners, 4),
            rows(owners, 1),
            rows(owners, 1),
            rows(shards, 1),
            rows(owners, 1),
            rows(shards, 4),
            rows(owners, 4),
            pltpu.SemaphoreType.DMA((5,)),
            pltpu.SemaphoreType.DMA((4,)),
            pltpu.SemaphoreType.DMA,
            pltpu.SemaphoreType.DMA((7,)),
            pltpu.SemaphoreType.DMA((7,)),
        ],
        compiler_params=pltpu.CompilerParams(
            collective_id=0, has_side_effects=True, vmem_limit_bytes=56 * 1024 * 1024
        ),
    )(gate_input, key_input, value_input, features, filter_weight, out_grad, *tables)


def solution(mesh):
    placed = (
        P("ch", "ctx"),
        P("ch", "ctx"),
        P("ch", "ctx"),
        P("ch", "ctx"),
        P(None, "ch"),
        P("ch", "ctx"),
    )
    return jax.shard_map(
        on_device,
        mesh=mesh,
        in_specs=placed,
        out_specs=(P("ch", "ctx"), P("ch", "ctx"), P("ch", "ctx"), P("ch", "ctx"), P(None, "ch")),
        check_vma=False,
    )
```

time: 472 us -> 56.7 us (0.12)
  blocking collectives: 310 us -> 0 us
  starting transfers between devices: 63.2 us -> 0 us
  waiting for transfers between devices: 61.6 us -> 0 us
  Pallas kernels: 0 us -> 51.8 us
  matrix products: 13.7 us -> 0 us
  local copies, waits for them, and re-layouts: 12 us -> 3.89 us
  other arithmetic: 6.92 us -> 0 us
    psum x1 -> x0, blocking collectives: 260 us -> none  [on_device(): weight_grad = lax.psum(partial_grad, 'ctx')]
    all_to_all x8 -> x0, starting transfers between devices: 63.2 us -> none  [the longest x2 36.1 us: to_spectrum(): lax.all_to_all(signal.reshape(1, length, columns), 'ctx', split_axis=1, c...]
    all_to_all x8 -> x0, waiting for transfers between devices: 61.6 us -> none  [the longest x2 19.8 us: to_time(): lax.all_to_all(jnp.stack([back_real, back_imag]), 'ctx', split_axis=2, co...]
    pallas_call x0 -> x1, Pallas kernels: none -> 51.8 us  [on_device(): pl.pallas_call(functools.partial(kernel, shards, groups), out_shape=(bloc...]
    all_gather x1 -> x0, blocking collectives: 50.2 us -> none  [on_device(): feats_all = lax.all_gather(features, 'ch', axis=0, tiled=True).T]
    dot_general x40 -> x0, matrix products: 13 us -> none  [the longest x4 1.27 us: local_dft(): jnp.einsum('kn,jnqw->jkqw', small_cos, real_view, precision=highest)]
  transfers between devices with their start and end apart: 8 -> 0, of which waited for: 7 -> 0; matrix products, arithmetic and copies ran while one was open for 4% -> 0% of each run, Pallas kernels for 0% -> 0%
where the time goes in v1:
time: 56.7 us; the launch traced here: 56.3 us
  Pallas kernels  51.8 us (91%)
  local copies, waits for them, and re-layouts  3.89 us (7%)
  between operations  0.65 us (1%)
    pallas_call x1, Pallas kernels, on_device(): pl.pallas_call(functools.partial(kernel, shards, groups), out_shape=(bloc...  51.8 us
    unnamed x13, local copies, waits for them, and re-layouts  3.89 us

profile of v1, /device:TPU:1, one launch (start us, length us, event | category | flops | bytes accessed | tf_op | source)
XLA Modules:
  0.0 56.3 jit_solution(8422095554674782801)
XLA Ops:
  0.6 51.8 %shard_map.137 = (bf16[64,128]{1,0:T(8,128)(2,1)}, bf16[64,128]{1,0:T(8,128)(2,1)}, bf16[64,128]{1,0:T(8,128)(2,1)}, bf16[64,128]{1,0:T(8,128)(2,1)}, f32[64,64]{1,0:T(8,128)}) custom-call(bf16[64,128]{1,0:T(8,128)(2,1)} %gate_in.1, bf16[64,128]{1,0:T(8,128)(2,1)} %key_in.1, bf16[64,128]{1,0:T(8,128)(2,1)} %value_in.1, f32[4,128]{1,0:T(4,128)} %feats_in.1, ...), custom_call_target="tpu_custom_call" | custom-call | tf_op jit(solution)/shard_map/pallas_call | solution.py:423
  52.4 0.0 copy-start.3
  52.5 1.3 %copy.20 = bf16[64,128]{1,0:T(8,128)(2,1)} copy(bf16[64,128]{1,0:T(8,128)(2,1)} %get-tuple-element.10) | data formatting | bytes 32768
  53.8 0.0 copy-done.3
  53.8 0.0 copy-start.2
  53.8 0.0 copy-start.1
  53.8 0.6 %copy.21 = bf16[64,128]{1,0:T(8,128)(2,1)} copy(bf16[64,128]{1,0:T(8,128)(2,1)S(1)} %copy-done.3) | data formatting | bytes 32768
  54.4 0.1 copy-done.2
  54.5 0.0 copy-start
  54.5 0.6 %copy.22 = bf16[64,128]{1,0:T(8,128)(2,1)} copy(bf16[64,128]{1,0:T(8,128)(2,1)S(1)} %copy-done.2) | data formatting | bytes 32768
  55.1 0.0 copy-done.1
  55.1 0.6 %copy.23 = bf16[64,128]{1,0:T(8,128)(2,1)} copy(bf16[64,128]{1,0:T(8,128)(2,1)S(1)} %copy-done.1) | data formatting | bytes 32768
  55.7 0.0 copy-done
  55.7 0.6 %copy.24 = f32[64,64]{1,0:T(8,128)} copy(f32[64,64]{1,0:T(8,128)S(1)} %copy-done) | data formatting | bytes 32768
Async XLA Ops:
  52.4 1.3 %copy-start.3 = (bf16[64,128]{1,0:T(8,128)(2,1)S(1)}, bf16[64,128]{1,0:T(8,128)(2,1)}, u32[]{:S(2)}) copy-start(bf16[64,128]{1,0:T(8,128)(2,1)} %get-tuple-element.11) | copy-start | bytes 49156
  53.8 0.7 %copy-start.2 = (bf16[64,128]{1,0:T(8,128)(2,1)S(1)}, bf16[64,128]{1,0:T(8,128)(2,1)}, u32[]{:S(2)}) copy-start(bf16[64,128]{1,0:T(8,128)(2,1)} %get-tuple-element.12) | copy-start | bytes 49156
  53.8 1.3 %copy-start.1 = (bf16[64,128]{1,0:T(8,128)(2,1)S(1)}, bf16[64,128]{1,0:T(8,128)(2,1)}, u32[]{:S(2)}) copy-start(bf16[64,128]{1,0:T(8,128)(2,1)} %get-tuple-element.13) | copy-start | bytes 49156
  54.5 1.2 %copy-start = (f32[64,64]{1,0:T(8,128)S(1)}, f32[64,64]{1,0:T(8,128)}, u32[]{:S(2)}) copy-start(f32[64,64]{1,0:T(8,128)} %get-tuple-element.14) | copy-start | bytes 49156

commit v2 on v1

--- a/solution.py
+++ b/solution.py
@@ -111,11 +111,8 @@
     last_in,
     mid_in,
     twist_in,
-    output,
-    gate_grad,
-    key_grad,
-    value_grad,
-    weight_grad,
+    recv_out,
+    recv_sum,
     gate,
     key,
     value,
@@ -138,14 +135,17 @@
     send_part,
     recv_part,
     send_sum,
-    recv_sum,
     send_out,
-    recv_out,
     in_sems,
     table_sems,
     own_sem,
+    feat_sems,
+    feat_sent,
     send_sems,
     recv_sems,
+    hello,
+    ready,
+    all_in,
 ):
     me = lax.axis_index("ctx")
     group = lax.axis_index("ch")
@@ -153,6 +153,18 @@
     chip = me // 2
     core = me % 2
     scaling = 1.0 / math.sqrt(shards * LANES)
+    deep = 4 if groups % 4 == 0 else 1
+    wide = groups // deep
+    rank = (group % deep) * wide + group // deep
+    kind = jnp.minimum(group % deep, 2)
+    known = wide * jnp.minimum(kind + 1, 2)
+    settled = jnp.minimum(wide * (kind + 1), groups)
+    greeters = known - jnp.where(kind < 2, 1, 0)
+    hub = 1
+    at_hub = chip == hub
+
+    def ranked(r):
+        return (r % wide) * deep + r // wide
 
     inputs = [
         pltpu.make_async_copy(src, dst, in_sems.at[n])
@@ -175,6 +187,9 @@
             device_id_type=MESH,
         ).start()
 
+    def tell(semaphore, where):
+        pl.semaphore_signal(semaphore, inc=1, device_id=where, device_id_type=MESH)
+
     def loop(low, high, step):
         def body(k, carry):
             step(k)
@@ -182,6 +197,14 @@
 
         lax.fori_loop(low, high, body, 0)
 
+    def others(low, high, step):
+        def guarded(r):
+            @pl.when(r != rank)
+            def _():
+                step(ranked(r))
+
+        loop(low, high, guarded)
+
     def arrived(ref, count, phase):
         part = ref.at[pl.ds(0, count)]
         pltpu.make_async_copy(part, part, recv_sems.at[phase]).wait()
@@ -194,40 +217,70 @@
         copy.start()
 
     barrier = pltpu.get_barrier_semaphore()
+    neighbour = {"ctx": me ^ 1, "ch": group}
+    even_feats, odd_feats = feats.at[group], feats.at[groups + group]
+    own_feats = pltpu.make_async_copy(feats_in, odd_feats, own_sem)
+
+    def push_feats(src, which, other):
+        pltpu.make_async_remote_copy(
+            src_ref=src,
+            dst_ref=feats.at[which * groups + group],
+            send_sem=feat_sent.at[which, other],
+            recv_sem=feat_sems.at[which, group],
+            device_id={"ctx": 2 * chip + 1, "ch": other},
+            device_id_type=MESH,
+        ).start()
+
+    def await_block(sems, which, other):
+        part = feats.at[which * groups + other]
+        pltpu.make_async_copy(part, part, sems.at[which, other]).wait()
+
+    def await_feats(other):
+        await_block(feat_sems, 0, other)
+        await_block(feat_sems, 1, other)
 
     @pl.when(core == 1)
     def _():
-        def tell(k):
-            pl.semaphore_signal(barrier, inc=1, device_id={"ctx": me ^ k, "ch": group}, device_id_type=MESH)
-
-        def tell_groups(k):
-            other = group ^ k
-            pl.semaphore_signal(barrier, inc=1, device_id={"ctx": me, "ch": other}, device_id_type=MESH)
-            pl.semaphore_signal(barrier, inc=1, device_id={"ctx": me - 1, "ch": other}, device_id_type=MESH)
-
-        loop(1, groups, tell_groups)
-        loop(1, shards, tell)
+        tell(barrier, neighbour)
+
+        @pl.when(jnp.logical_not(at_hub))
+        def _():
+            tell(barrier, {"ctx": 2 * hub, "ch": group})
+
+        def greet(other):
+            tell(barrier, {"ctx": me, "ch": other})
+
+            @pl.when(jnp.logical_not(at_hub))
+            def _():
+                tell(barrier, {"ctx": me - 1, "ch": other})
+
+        others(jnp.where(kind < 2, wide * kind, groups), groups, greet)
+        pl.semaphore_wait(barrier, greeters + jnp.where(at_hub, 1, 0))
+        others(0, known, lambda other: push_feats(feats_in, 1, other))
+        own_feats.start()
         for copy in tables:
             copy.start()
-        pl.semaphore_wait(barrier, owners - 1 + groups - 1)
-
-    @pl.when(core == 0)
-    def _():
-        pl.semaphore_wait(barrier, owners + groups - 1)
-
-    def push_feats(k):
-        push(feats_in, feats.at[core * groups + group], 0, {"ctx": 2 * chip + 1, "ch": group ^ k})
-
-    loop(1, groups, push_feats)
-    own_feats = pltpu.make_async_copy(feats_in, feats.at[core * groups + group], own_sem)
-
-    @pl.when(core == 0)
-    def _():
-        push_feats(0)
-
-    @pl.when(core == 1)
-    def _():
-        own_feats.start()
+
+        @pl.when(at_hub)
+        def _():
+            tell(hello, neighbour)
+            await_block(feat_sems, 0, group)
+            others(0, known, lambda other: push_feats(even_feats, 0, other))
+
+    @pl.when(jnp.logical_and(core == 0, at_hub))
+    def _():
+        tell(barrier, neighbour)
+        pl.semaphore_wait(hello, 1)
+        push_feats(feats_in, 0, group)
+
+        pl.semaphore_wait(barrier, owners)
+        loop(0, owners, lambda k: tell(ready, {"ctx": 2 * k + 1, "ch": group}))
+
+    @pl.when(jnp.logical_and(core == 0, jnp.logical_not(at_hub)))
+    def _():
+        pl.semaphore_wait(barrier, greeters + 1)
+        others(0, known, lambda other: push_feats(feats_in, 0, other))
+        push_feats(feats_in, 0, group)
 
     for copy in inputs[:4]:
         copy.wait()
@@ -243,17 +296,27 @@
         to = chip ^ k
         push(send_sig.at[to], recv_sig.at[me], 1, {"ctx": 2 * to + 1, "ch": group})
 
-    loop(1, owners, push_sig)
-
     @pl.when(core == 0)
     def _():
-        push_sig(0)
+        @pl.when(jnp.logical_not(at_hub))
+        def _():
+            pl.semaphore_wait(ready, 1)
+
+        loop(0, owners, push_sig)
 
     inputs[4].wait()
 
     @pl.when(core == 1)
     def _():
         recv_sig[pl.ds(me, 1)] = send_sig[pl.ds(chip, 1)]
+        pl.semaphore_wait(ready, 1)
+        loop(1, owners, push_sig)
+
+        @pl.when(jnp.logical_not(at_hub))
+        def _():
+            await_block(feat_sems, 0, group)
+            tell(ready, neighbour)
+
         eye = (
             lax.broadcasted_iota(jnp.int32, (2 * owners, 2 * owners), 0)
             == lax.broadcasted_iota(jnp.int32, (2 * owners, 2 * owners), 1)
@@ -272,7 +335,54 @@
         lasts = [(last_split[0], last_split[1]), (last_split[2], last_split[3])]
 
         own_feats.wait()
-        arrived(feats, 2 * groups - 1, 0)
+
+        def push_both(other):
+            push_feats(even_feats, 0, other)
+            push_feats(odd_feats, 1, other)
+
+        @pl.when(kind == 2)
+        def _():
+            pl.semaphore_wait(all_in, 1)
+            others(known, groups, push_both)
+
+        arrived(recv_sig, shards - 1, 1)
+        specs = spectra([recv_sig[:, n, :] for n in range(4)], first_split[0], forward, cos, sin)
+        mixed_specs = [specs[:rows], specs[rows : 2 * rows]]
+        inner_specs = [specs[2 * rows : 3 * rows], specs[3 * rows :]]
+        taps = signals_of(
+            [times_conj(inner_specs[n], mixed_specs[n]) for n in range(2)], lasts[1], backward, cos, sin
+        )
+        send_taps[:, 0, :] = taps[:owners, :LANES]
+        send_taps[:, 1, :] = taps[owners:, :LANES]
+        send_taps[:, 2, :] = taps[:owners, LANES:]
+        send_taps[:, 3, :] = taps[owners:, LANES:]
+
+        def push_taps(k):
+            to = chip ^ k
+            push(send_taps.at[to], recv_taps.at[chip], 3, {"ctx": 2 * to + 1, "ch": group})
+
+        loop(1, owners, push_taps)
+        recv_taps[pl.ds(chip, 1)] = send_taps[pl.ds(chip, 1)]
+
+        def trade(other):
+            await_feats(other)
+            push_both(other)
+
+        @pl.when(kind < 2)
+        def _():
+            others(0, settled, await_feats)
+            others(settled, groups, trade)
+
+        @pl.when(jnp.logical_and(kind == 0, 2 * wide < groups))
+        def _():
+            for step in range(2, deep):
+                tell(all_in, {"ctx": me, "ch": group + step})
+
+        @pl.when(kind == 2)
+        def _():
+            others(0, known, await_feats)
+            others(known, groups, await_feats)
+
         per = feats.shape[1]
         feats_all = jnp.concatenate(
             [
@@ -294,24 +404,29 @@
         loop(1, owners, push_filt)
         recv_filt[pl.ds(chip, 1)] = send_filt[pl.ds(chip, 1)]
 
-        arrived(recv_sig, shards - 1, 1)
-        specs = spectra([recv_sig[:, n, :] for n in range(4)], first_split[0], forward, cos, sin)
-        mixed_specs = [specs[:rows], specs[rows : 2 * rows]]
-        inner_specs = [specs[2 * rows : 3 * rows], specs[3 * rows :]]
-        taps = signals_of(
-            [times_conj(inner_specs[n], mixed_specs[n]) for n in range(2)], lasts[1], backward, cos, sin
-        )
-        send_taps[:, 0, :] = taps[:owners, :LANES]
-        send_taps[:, 1, :] = taps[owners:, :LANES]
-        send_taps[:, 2, :] = taps[:owners, LANES:]
-        send_taps[:, 3, :] = taps[owners:, LANES:]
-
-        def push_taps(k):
+        def sent_odd(other):
+            await_block(feat_sent, 1, other)
+
+        others(0, groups, sent_odd)
+        others(jnp.where(at_hub, 0, known), groups, lambda other: await_block(feat_sent, 0, other))
+
+        arrived(recv_taps, owners - 1, 3)
+        taps_here = jnp.concatenate(
+            [
+                jnp.concatenate([recv_taps[:, 0, :], recv_taps[:, 1, :]], axis=1),
+                jnp.concatenate([recv_taps[:, 2, :], recv_taps[:, 3, :]], axis=1),
+            ],
+            axis=0,
+        )
+        part = dot_t(taps_here, feats_all)
+        send_part[:, 0, :] = jnp.concatenate([part[:owners], part[owners:]], axis=1)
+
+        def push_part(k):
             to = chip ^ k
-            push(send_taps.at[to], recv_taps.at[chip], 3, {"ctx": 2 * to + 1, "ch": group})
-
-        loop(1, owners, push_taps)
-        recv_taps[pl.ds(chip, 1)] = send_taps[pl.ds(chip, 1)]
+            push(send_part.at[to], recv_part.at[chip], 5, {"ctx": 2 * to + 1, "ch": group})
+
+        loop(1, owners, push_part)
+        recv_part[pl.ds(chip, 1)] = send_part[pl.ds(chip, 1)]
 
         arrived(recv_filt, owners - 1, 2)
         filt_specs = spectra(
@@ -343,24 +458,6 @@
         loop(1, shards, push_out)
         recv_out[pl.ds(chip, 1)] = send_out[pl.ds(me, 1)]
 
-        arrived(recv_taps, owners - 1, 3)
-        taps_here = jnp.concatenate(
-            [
-                jnp.concatenate([recv_taps[:, 0, :], recv_taps[:, 1, :]], axis=1),
-                jnp.concatenate([recv_taps[:, 2, :], recv_taps[:, 3, :]], axis=1),
-            ],
-            axis=0,
-        )
-        part = dot_t(taps_here, feats_all)
-        send_part[:, 0, :] = jnp.concatenate([part[:owners], part[owners:]], axis=1)
-
-        def push_part(k):
-            to = chip ^ k
-            push(send_part.at[to], recv_part.at[chip], 5, {"ctx": 2 * to + 1, "ch": group})
-
-        loop(1, owners, push_part)
-        recv_part[pl.ds(chip, 1)] = send_part[pl.ds(chip, 1)]
-
         arrived(recv_part, owners - 1, 5)
         send_sum[pl.ds(0, 1)] = jnp.sum(recv_part[...], axis=0, keepdims=True) * (scaling * scaling)
 
@@ -374,34 +471,39 @@
         sent(send_taps, owners - 1, 3)
         sent(send_out, shards - 1, 4)
         sent(send_part, owners - 1, 5)
-        sent(feats, groups - 1, 0)
         sent(send_sig, owners - 1, 1)
 
     @pl.when(core == 0)
     def _():
         arrived(recv_out, owners, 4)
-        sent(feats, groups, 0)
+        await_block(feat_sent, 0, group)
+
+        @pl.when(jnp.logical_not(at_hub))
+        def _():
+            others(0, known, lambda other: await_block(feat_sent, 0, other))
+
         sent(send_sig, owners, 1)
 
-    conv = jnp.concatenate([recv_out[:, 0, :], recv_out[:, 1, :]], axis=0)
-    mixed_grad = jnp.concatenate([recv_out[:, 2, :], recv_out[:, 3, :]], axis=0)
+    @pl.when(core == 1)
+    def _():
+        arrived(recv_sum, owners - 1, 6)
+        sent(send_sum, shards - 1, 6)
+
+    @pl.when(core == 0)
+    def _():
+        arrived(recv_sum, owners, 6)
+
+
+def finish(gate, key, value, upstream, out, total, output, gate_grad, key_grad, value_grad, weight_grad):
+    conv = jnp.concatenate([out[:, 0, :], out[:, 1, :]], axis=0)
+    mixed_grad = jnp.concatenate([out[:, 2, :], out[:, 3, :]], axis=0)
     output[...] = (gate[...].astype(f32) * conv).astype(bf16)
     gate_grad[...] = (upstream[...].astype(f32) * conv).astype(bf16)
     key_grad[...] = (mixed_grad * value[...].astype(f32)).astype(bf16)
     value_grad[...] = (mixed_grad * key[...].astype(f32)).astype(bf16)
-
-    @pl.when(core == 1)
-    def _():
-        arrived(recv_sum, owners - 1, 6)
-        sent(send_sum, shards - 1, 6)
-
-    @pl.when(core == 0)
-    def _():
-        arrived(recv_sum, owners, 6)
-
-    total = recv_sum[:, 0, :]
-    half = total.shape[1] // 2
-    grad_rows = jnp.concatenate([total[:, :half], total[:, half:]], axis=0)
+    sums = total[:, 0, :]
+    half = sums.shape[1] // 2
+    grad_rows = jnp.concatenate([sums[:, :half], sums[:, half:]], axis=0)
     eye = (
         lax.broadcasted_iota(jnp.int32, (half, half), 0) == lax.broadcasted_iota(jnp.int32, (half, half), 1)
     ).astype(f32)
@@ -420,11 +522,14 @@
     rows = lambda count, width: pltpu.VMEM((count, width, LANES), f32)
     block = jax.ShapeDtypeStruct((channels, length), bf16)
     per = features.shape[0]
-    return pl.pallas_call(
+    out, total = pl.pallas_call(
         functools.partial(kernel, shards, groups),
-        out_shape=(block, block, block, block, jax.ShapeDtypeStruct((feat, channels), f32)),
+        out_shape=(
+            jax.ShapeDtypeStruct((owners, 4, LANES), f32),
+            jax.ShapeDtypeStruct((owners, 1, LANES), f32),
+        ),
         in_specs=[hbm] * 10,
-        out_specs=(vmem,) * 5,
+        out_specs=(vmem,) * 2,
         scratch_shapes=[
             *[pltpu.VMEM((channels, length), bf16)] * 4,
             pltpu.VMEM(filter_weight.shape, f32),
@@ -442,19 +547,28 @@
             rows(owners, 1),
             rows(owners, 1),
             rows(shards, 1),
-            rows(owners, 1),
             rows(shards, 4),
-            rows(owners, 4),
             pltpu.SemaphoreType.DMA((5,)),
             pltpu.SemaphoreType.DMA((4,)),
             pltpu.SemaphoreType.DMA,
+            pltpu.SemaphoreType.DMA((2, groups)),
+            pltpu.SemaphoreType.DMA((2, groups)),
             pltpu.SemaphoreType.DMA((7,)),
             pltpu.SemaphoreType.DMA((7,)),
+            pltpu.SemaphoreType.REGULAR,
+            pltpu.SemaphoreType.REGULAR,
+            pltpu.SemaphoreType.REGULAR,
         ],
         compiler_params=pltpu.CompilerParams(
             collective_id=0, has_side_effects=True, vmem_limit_bytes=56 * 1024 * 1024
         ),
     )(gate_input, key_input, value_input, features, filter_weight, out_grad, *tables)
+    return pl.pallas_call(
+        finish,
+        out_shape=(block, block, block, block, jax.ShapeDtypeStruct((feat, channels), f32)),
+        in_specs=[vmem] * 6,
+        out_specs=(vmem,) * 5,
+    )(gate_input, key_input, value_input, out_grad, out, total)
 
 
 def solution(mesh):

time: 56.7 us -> 43.3 us (0.76)
  Pallas kernels: 51.8 us -> 42.4 us
  local copies, waits for them, and re-layouts: 3.89 us -> 0 us
    pallas_call x1 -> x2, Pallas kernels: 51.8 us -> 42.4 us  [the longest x1 40.6 us: on_device(): pl.pallas_call(functools.partial(kernel, shards, groups), out_shape=(jax....]
    unnamed x13 -> x0, local copies, waits for them, and re-layouts: 3.89 us -> none
where the time goes in v2:
time: 43.3 us; the launch traced here: 43 us
  Pallas kernels  42.4 us (98%)
  between operations  0.64 us (1%)
    pallas_call x1, Pallas kernels, on_device(): pl.pallas_call(functools.partial(kernel, shards, groups), out_shape=(jax....  40.6 us
    pallas_call x1, Pallas kernels, on_device(): pl.pallas_call(finish, out_shape=(block, block, block, block, jax.ShapeDt...  1.79 us

profile of v2, /device:TPU:1, one launch (start us, length us, event | category | flops | bytes accessed | tf_op | source)
XLA Modules:
  0.0 43.0 jit_solution(14378737723400654681)
XLA Ops:
  0.6 40.6 %shard_map.137 = (f32[32,4,128]{2,1,0:T(4,128)}, f32[32,1,128]{2,1,0:T(1,128)}) custom-call(bf16[64,128]{1,0:T(8,128)(2,1)} %gate.1, bf16[64,128]{1,0:T(8,128)(2,1)} %key.1, bf16[64,128]{1,0:T(8,128)(2,1)} %value.1, f32[4,128]{1,0:T(4,128)} %feats_in.1, f32[64,64]{1,0:T(8,128)} %weight_in.1, bf16[64,128]{1,0:T(8,128)(2,1)} %upstream.1, ...), custom_call_target="tpu_custom_call" | custom-call | tf_op jit(solution)/shard_map/pallas_call | solution.py:525
  41.2 1.8 %shard_map.138 = (bf16[64,128]{1,0:T(8,128)(2,1)}, bf16[64,128]{1,0:T(8,128)(2,1)}, bf16[64,128]{1,0:T(8,128)(2,1)}, bf16[64,128]{1,0:T(8,128)(2,1)}, f32[64,64]{1,0:T(8,128)}) custom-call(bf16[64,128]{1,0:T(8,128)(2,1)} %gate.1, bf16[64,128]{1,0:T(8,128)(2,1)} %key.1, bf16[64,128]{1,0:T(8,128)(2,1)} %value.1, bf16[64,128]{1,0:T(8,128)(2,1)} %upstream.1, ...), custom_call_target="tpu_custom_call" | custom-call | tf_op jit(solution)/shard_map/pallas_call | solution.py:566

commit v3 on v2

--- a/solution.py
+++ b/solution.py
@@ -126,6 +126,7 @@
     last_split,
     mid_split,
     feats,
+    feats_all,
     send_sig,
     recv_sig,
     send_filt,
@@ -158,10 +159,13 @@
     rank = (group % deep) * wide + group // deep
     kind = jnp.minimum(group % deep, 2)
     known = wide * jnp.minimum(kind + 1, 2)
-    settled = jnp.minimum(wide * (kind + 1), groups)
+    settled = min(2 * wide, groups)
     greeters = known - jnp.where(kind < 2, 1, 0)
     hub = 1
     at_hub = chip == hub
+    reducers = owners // 2
+    reducer = jnp.logical_and(core == 1, jnp.logical_or(chip % 4 == 1, chip % 4 == 2))
+    my_reducer = chip // 4 * 2 + chip % 4 - 1
 
     def ranked(r):
         return (r % wide) * deep + r // wide
@@ -197,6 +201,10 @@
 
         lax.fori_loop(low, high, body, 0)
 
+    def far_first(low, count, step):
+        loop(count // 2, count, step)
+        loop(low, count // 2, step)
+
     def others(low, high, step):
         def guarded(r):
             @pl.when(r != rank)
@@ -279,6 +287,11 @@
     @pl.when(jnp.logical_and(core == 0, jnp.logical_not(at_hub)))
     def _():
         pl.semaphore_wait(barrier, greeters + 1)
+
+        @pl.when(jnp.logical_not(at_hub))
+        def _():
+            tell(hello, neighbour)
+
         others(0, known, lambda other: push_feats(feats_in, 0, other))
         push_feats(feats_in, 0, group)
 
@@ -302,7 +315,7 @@
         def _():
             pl.semaphore_wait(ready, 1)
 
-        loop(0, owners, push_sig)
+        far_first(0, owners, push_sig)
 
     inputs[4].wait()
 
@@ -310,11 +323,12 @@
     def _():
         recv_sig[pl.ds(me, 1)] = send_sig[pl.ds(chip, 1)]
         pl.semaphore_wait(ready, 1)
-        loop(1, owners, push_sig)
+
+        far_first(1, owners, push_sig)
 
         @pl.when(jnp.logical_not(at_hub))
         def _():
-            await_block(feat_sems, 0, group)
+            pl.semaphore_wait(hello, 1)
             tell(ready, neighbour)
 
         eye = (
@@ -336,6 +350,10 @@
 
         own_feats.wait()
 
+        @pl.when(jnp.logical_not(at_hub))
+        def _():
+            await_block(feat_sems, 0, group)
+
         def push_both(other):
             push_feats(even_feats, 0, other)
             push_feats(odd_feats, 1, other)
@@ -344,6 +362,54 @@
         def _():
             pl.semaphore_wait(all_in, 1)
             others(known, groups, push_both)
+
+        def trade(other):
+            await_feats(other)
+            push_both(other)
+
+        def push_filt(k):
+            to = chip ^ k
+            push(send_filt.at[to], recv_filt.at[chip], 2, {"ctx": 2 * to + 1, "ch": group})
+
+        def filter_phase():
+            @pl.when(kind == 0)
+            def _():
+                others(2 * wide, groups, trade)
+
+                @pl.when(2 * wide < groups)
+                def _():
+                    for step in range(2, deep):
+                        tell(all_in, {"ctx": me, "ch": group + step})
+
+            @pl.when(kind == 1)
+            def _():
+                others(0, settled, await_feats)
+                others(settled, groups, trade)
+
+            @pl.when(kind == 2)
+            def _():
+                others(0, groups, await_feats)
+
+            per = feats.shape[1]
+            feats_all[...] = jnp.concatenate(
+                [
+                    feats[:groups].reshape(groups * per, LANES),
+                    feats[groups:].reshape(groups * per, LANES),
+                ],
+                axis=1,
+            )
+            filt = jnp.dot(weight_t, feats_all[...], precision=HIGHEST, preferred_element_type=f32) * scaling
+            send_filt[:, 0, :] = filt[:owners, :LANES]
+            send_filt[:, 1, :] = filt[:owners, LANES:]
+            send_filt[:, 2, :] = filt[owners:, :LANES]
+            send_filt[:, 3, :] = filt[owners:, LANES:]
+            far_first(1, owners, push_filt)
+            recv_filt[pl.ds(chip, 1)] = send_filt[pl.ds(chip, 1)]
+
+        @pl.when(kind == 0)
+        def _():
+            others(0, wide, await_feats)
+            others(wide, jnp.minimum(2 * wide, groups), trade)
 
         arrived(recv_sig, shards - 1, 1)
         specs = spectra([recv_sig[:, n, :] for n in range(4)], first_split[0], forward, cos, sin)
@@ -361,54 +427,10 @@
             to = chip ^ k
             push(send_taps.at[to], recv_taps.at[chip], 3, {"ctx": 2 * to + 1, "ch": group})
 
-        loop(1, owners, push_taps)
+        far_first(1, owners, push_taps)
         recv_taps[pl.ds(chip, 1)] = send_taps[pl.ds(chip, 1)]
 
-        def trade(other):
-            await_feats(other)
-            push_both(other)
-
-        @pl.when(kind < 2)
-        def _():
-            others(0, settled, await_feats)
-            others(settled, groups, trade)
-
-        @pl.when(jnp.logical_and(kind == 0, 2 * wide < groups))
-        def _():
-            for step in range(2, deep):
-                tell(all_in, {"ctx": me, "ch": group + step})
-
-        @pl.when(kind == 2)
-        def _():
-            others(0, known, await_feats)
-            others(known, groups, await_feats)
-
-        per = feats.shape[1]
-        feats_all = jnp.concatenate(
-            [
-                feats[:groups].reshape(groups * per, LANES),
-                feats[groups:].reshape(groups * per, LANES),
-            ],
-            axis=1,
-        )
-        filt = jnp.dot(weight_t, feats_all, precision=HIGHEST, preferred_element_type=f32) * scaling
-        send_filt[:, 0, :] = filt[:owners, :LANES]
-        send_filt[:, 1, :] = filt[:owners, LANES:]
-        send_filt[:, 2, :] = filt[owners:, :LANES]
-        send_filt[:, 3, :] = filt[owners:, LANES:]
-
-        def push_filt(k):
-            to = chip ^ k
-            push(send_filt.at[to], recv_filt.at[chip], 2, {"ctx": 2 * to + 1, "ch": group})
-
-        loop(1, owners, push_filt)
-        recv_filt[pl.ds(chip, 1)] = send_filt[pl.ds(chip, 1)]
-
-        def sent_odd(other):
-            await_block(feat_sent, 1, other)
-
-        others(0, groups, sent_odd)
-        others(jnp.where(at_hub, 0, known), groups, lambda other: await_block(feat_sent, 0, other))
+        filter_phase()
 
         arrived(recv_taps, owners - 1, 3)
         taps_here = jnp.concatenate(
@@ -418,15 +440,22 @@
             ],
             axis=0,
         )
-        part = dot_t(taps_here, feats_all)
-        send_part[:, 0, :] = jnp.concatenate([part[:owners], part[owners:]], axis=1)
+        part = dot_t(taps_here, feats_all[...])
+        pairs = jnp.concatenate([part[:owners], part[owners:]], axis=1)
+        send_part[:, 0, :] = pairs[:reducers]
+        send_part[:, 1, :] = pairs[reducers:]
 
         def push_part(k):
-            to = chip ^ k
-            push(send_part.at[to], recv_part.at[chip], 5, {"ctx": 2 * to + 1, "ch": group})
-
-        loop(1, owners, push_part)
-        recv_part[pl.ds(chip, 1)] = send_part[pl.ds(chip, 1)]
+            @pl.when(jnp.logical_not(jnp.logical_and(reducer, k == my_reducer)))
+            def _():
+                to = k // 2 * 4 + 1 + k % 2
+                push(send_part.at[k], recv_part.at[chip], 5, {"ctx": 2 * to + 1, "ch": group})
+
+        loop(0, reducers, push_part)
+
+        @pl.when(reducer)
+        def _():
+            recv_part[pl.ds(chip, 1)] = send_part[pl.ds(my_reducer, 1)]
 
         arrived(recv_filt, owners - 1, 2)
         filt_specs = spectra(
@@ -455,23 +484,36 @@
             to = me ^ k
             push(send_out.at[to], recv_out.at[chip], 4, {"ctx": to, "ch": group})
 
-        loop(1, shards, push_out)
+        far_first(1, shards, push_out)
         recv_out[pl.ds(chip, 1)] = send_out[pl.ds(me, 1)]
 
-        arrived(recv_part, owners - 1, 5)
-        send_sum[pl.ds(0, 1)] = jnp.sum(recv_part[...], axis=0, keepdims=True) * (scaling * scaling)
-
-        def push_sum(k):
-            push(send_sum.at[0], recv_sum.at[chip], 6, {"ctx": me ^ k, "ch": group})
-
-        loop(1, shards, push_sum)
-        recv_sum[pl.ds(chip, 1)] = send_sum[pl.ds(0, 1)]
-        arrived(recv_out, owners - 1, 4)
+        def sent_odd(other):
+            await_block(feat_sent, 1, other)
+
+        others(0, groups, sent_odd)
+        others(jnp.where(at_hub, 0, known), groups, lambda other: await_block(feat_sent, 0, other))
         sent(send_filt, owners - 1, 2)
         sent(send_taps, owners - 1, 3)
+        sent(send_sig, owners - 1, 1)
+
+        @pl.when(reducer)
+        def _():
+            arrived(recv_part, owners - 1, 5)
+            send_sum[pl.ds(0, 1)] = jnp.sum(recv_part[...], axis=0, keepdims=True) * (scaling * scaling)
+
+            def push_sum(k):
+                push(send_sum.at[0], recv_sum.at[my_reducer], 6, {"ctx": me ^ k, "ch": group})
+
+            far_first(1, shards, push_sum)
+            recv_sum[pl.ds(my_reducer, 1)] = send_sum[pl.ds(0, 1)]
+            sent(send_part, reducers - 1, 5)
+
+        @pl.when(jnp.logical_not(reducer))
+        def _():
+            sent(send_part, reducers, 5)
+
+        arrived(recv_out, owners - 1, 4)
         sent(send_out, shards - 1, 4)
-        sent(send_part, owners - 1, 5)
-        sent(send_sig, owners - 1, 1)
 
     @pl.when(core == 0)
     def _():
@@ -486,28 +528,54 @@
 
     @pl.when(core == 1)
     def _():
-        arrived(recv_sum, owners - 1, 6)
-        sent(send_sum, shards - 1, 6)
+        @pl.when(reducer)
+        def _():
+            arrived(recv_sum, reducers - 1, 6)
+            sent(send_sum, shards - 1, 6)
+
+        @pl.when(jnp.logical_not(reducer))
+        def _():
+            arrived(recv_sum, reducers, 6)
 
     @pl.when(core == 0)
     def _():
-        arrived(recv_sum, owners, 6)
-
-
-def finish(gate, key, value, upstream, out, total, output, gate_grad, key_grad, value_grad, weight_grad):
+        arrived(recv_sum, reducers, 6)
+
+
+def finish(*refs):
+    sources, targets = refs[:6], refs[6:11]
+    gate, key, value, upstream, out, total = refs[11:17]
+    results = refs[17:22]
+    in_sems, out_sems = refs[22:]
+    loads = [
+        pltpu.make_async_copy(source, ref, in_sems.at[n])
+        for n, (source, ref) in enumerate(zip(sources, (gate, key, value, upstream, out, total)))
+    ]
+    stores = [
+        pltpu.make_async_copy(ref, target, out_sems.at[n]) for n, (ref, target) in enumerate(zip(results, targets))
+    ]
+    for n in (4, 0, 3, 1, 2, 5):
+        loads[n].start()
+    loads[4].wait()
     conv = jnp.concatenate([out[:, 0, :], out[:, 1, :]], axis=0)
     mixed_grad = jnp.concatenate([out[:, 2, :], out[:, 3, :]], axis=0)
-    output[...] = (gate[...].astype(f32) * conv).astype(bf16)
-    gate_grad[...] = (upstream[...].astype(f32) * conv).astype(bf16)
-    key_grad[...] = (mixed_grad * value[...].astype(f32)).astype(bf16)
-    value_grad[...] = (mixed_grad * key[...].astype(f32)).astype(bf16)
-    sums = total[:, 0, :]
+    for n, (load, ref, factor) in enumerate(
+        [(0, gate, conv), (3, upstream, conv), (2, value, mixed_grad), (1, key, mixed_grad)]
+    ):
+        loads[load].wait()
+        results[n][...] = (ref[...].astype(f32) * factor).astype(bf16)
+        stores[n].start()
+    loads[5].wait()
+    sums = jnp.concatenate([total[:, 0, :], total[:, 1, :]], axis=0)
     half = sums.shape[1] // 2
     grad_rows = jnp.concatenate([sums[:, :half], sums[:, half:]], axis=0)
     eye = (
         lax.broadcasted_iota(jnp.int32, (half, half), 0) == lax.broadcasted_iota(jnp.int32, (half, half), 1)
     ).astype(f32)
-    weight_grad[...] = dot_t(eye, grad_rows)
+    results[4][...] = dot_t(eye, grad_rows)
+    stores[4].start()
+    for store in stores:
+        store.wait()
 
 
 def on_device(gate_input, key_input, value_input, features, filter_weight, out_grad):
@@ -515,6 +583,7 @@
     channels, length = gate_input.shape
     feat = filter_weight.shape[0]
     owners = shards // 2
+    reducers = owners // 2
     assert channels == 2 * owners and length == LANES and feat == LANES // 2
     tables = make_tables(shards)
     hbm = pl.BlockSpec(memory_space=pl.ANY)
@@ -526,7 +595,7 @@
         functools.partial(kernel, shards, groups),
         out_shape=(
             jax.ShapeDtypeStruct((owners, 4, LANES), f32),
-            jax.ShapeDtypeStruct((owners, 1, LANES), f32),
+            jax.ShapeDtypeStruct((reducers, 2, LANES), f32),
         ),
         in_specs=[hbm] * 10,
         out_specs=(vmem,) * 2,
@@ -538,15 +607,16 @@
             pltpu.VMEM((4, *tables[1].shape[1:]), bf16),
             pltpu.VMEM((4, *tables[2].shape[1:]), bf16),
             rows(2 * groups, per),
+            pltpu.VMEM((feat, 2 * LANES), f32),
             rows(owners, 4),
             rows(shards, 4),
             rows(owners, 4),
             rows(owners, 4),
             rows(owners, 4),
             rows(owners, 4),
-            rows(owners, 1),
-            rows(owners, 1),
-            rows(shards, 1),
+            rows(reducers, 2),
+            rows(owners, 2),
+            rows(shards, 2),
             rows(shards, 4),
             pltpu.SemaphoreType.DMA((5,)),
             pltpu.SemaphoreType.DMA((4,)),
@@ -566,8 +636,18 @@
     return pl.pallas_call(
         finish,
         out_shape=(block, block, block, block, jax.ShapeDtypeStruct((feat, channels), f32)),
-        in_specs=[vmem] * 6,
-        out_specs=(vmem,) * 5,
+        in_specs=[hbm] * 6,
+        out_specs=(hbm,) * 5,
+        scratch_shapes=[
+            *[pltpu.VMEM((channels, length), bf16)] * 4,
+            rows(owners, 4),
+            rows(reducers, 2),
+            *[pltpu.VMEM((channels, length), bf16)] * 4,
+            pltpu.VMEM((feat, channels), f32),
+            pltpu.SemaphoreType.DMA((6,)),
+            pltpu.SemaphoreType.DMA((5,)),
+        ],
+        compiler_params=pltpu.CompilerParams(vmem_limit_bytes=56 * 1024 * 1024),
     )(gate_input, key_input, value_input, out_grad, out, total)
 
 

time: 43.3 us -> 42.4 us (0.979)
  Pallas kernels: 42.4 us -> 41.5 us
    pallas_call x1, Pallas kernels: 40.6 us -> 39.7 us  [on_device(): pl.pallas_call(functools.partial(kernel, shards, groups), out_shape=(jax....]
where the time goes in v3:
time: 42.4 us; the launch traced here: 42.2 us
  Pallas kernels  41.5 us (98%)
  between operations  0.64 us (2%)
    pallas_call x1, Pallas kernels, on_device(): pl.pallas_call(functools.partial(kernel, shards, groups), out_shape=(jax....  39.7 us
    pallas_call x1, Pallas kernels, on_device(): pl.pallas_call(finish, out_shape=(block, block, block, block, jax.ShapeDt...  1.87 us

profile of v3, /device:TPU:1, one launch (start us, length us, event | category | flops | bytes accessed | tf_op | source)
XLA Modules:
  0.0 42.2 jit_solution(11727641255752290274)
XLA Ops:
  0.6 39.7 %shard_map.137 = (f32[32,4,128]{2,1,0:T(4,128)}, f32[16,2,128]{2,1,0:T(2,128)}) custom-call(bf16[64,128]{1,0:T(8,128)(2,1)} %refs_0_.1, bf16[64,128]{1,0:T(8,128)(2,1)} %refs_1_.1, bf16[64,128]{1,0:T(8,128)(2,1)} %refs_2_.1, f32[4,128]{1,0:T(4,128)} %feats_in.1, f32[64,64]{1,0:T(8,128)} %weight_in.1, bf16[64,128]{1,0:T(8,128)(2,1)} %refs_3_.1, ...), custom_call_target="tpu_custom_call" | custom-call | tf_op jit(solution)/shard_map/pallas_call | solution.py:594
  40.3 1.9 %shard_map.138 = (bf16[64,128]{1,0:T(8,128)(2,1)}, bf16[64,128]{1,0:T(8,128)(2,1)}, bf16[64,128]{1,0:T(8,128)(2,1)}, bf16[64,128]{1,0:T(8,128)(2,1)}, f32[64,64]{1,0:T(8,128)}) custom-call(bf16[64,128]{1,0:T(8,128)(2,1)} %refs_0_.1, bf16[64,128]{1,0:T(8,128)(2,1)} %refs_1_.1, bf16[64,128]{1,0:T(8,128)(2,1)} %refs_2_.1, bf16[64,128]{1,0:T(8,128)(2,1)} %refs_3_.1, ...), custom_call_target="tpu_custom_call" | custom-call | tf_op jit(solution)/shard_map/pallas_call | solution.py:636

commit v4 on v3

--- a/solution.py
+++ b/solution.py
@@ -56,6 +56,10 @@
     return jnp.dot(a, b, preferred_element_type=f32)
 
 
+def rows_by_rows(a, b):
+    return lax.dot_general(a, b, (((1,), (1,)), ((), ())), preferred_element_type=f32)
+
+
 def dot_t(a, b):
     return lax.dot_general(a, b, (((1,), (1,)), ((), ())), precision=HIGHEST, preferred_element_type=f32)
 
@@ -111,6 +115,16 @@
     last_in,
     mid_in,
     twist_in,
+    output_hbm,
+    gate_grad_hbm,
+    key_grad_hbm,
+    value_grad_hbm,
+    weight_grad_hbm,
+    output,
+    gate_grad,
+    key_grad,
+    value_grad,
+    weight_grad,
     recv_out,
     recv_sum,
     gate,
@@ -138,6 +152,7 @@
     send_sum,
     send_out,
     in_sems,
+    out_sems,
     table_sems,
     own_sem,
     feat_sems,
@@ -163,9 +178,18 @@
     greeters = known - jnp.where(kind < 2, 1, 0)
     hub = 1
     at_hub = chip == hub
-    reducers = owners // 2
-    reducer = jnp.logical_and(core == 1, jnp.logical_or(chip % 4 == 1, chip % 4 == 2))
-    my_reducer = chip // 4 * 2 + chip % 4 - 1
+    reducers = owners // 4
+    ring = owners // 4
+    along = chip // 4
+    nearness = jnp.where(
+        along < 2, along, jnp.where(along == ring - 1, 2, jnp.where(along == 2, 3, reducers))
+    )
+    my_reducer = nearness * 2 + chip % 4
+    reducer = jnp.logical_and(core == 1, jnp.logical_and(chip % 4 < 2, my_reducer < reducers))
+
+    def reducer_chip(k):
+        near = k // 2
+        return jnp.where(near == 2, ring - 1, jnp.where(near == 3, 2, near)) * 4 + k % 2
 
     def ranked(r):
         return (r % wide) * deep + r // wide
@@ -335,7 +359,8 @@
             lax.broadcasted_iota(jnp.int32, (2 * owners, 2 * owners), 0)
             == lax.broadcasted_iota(jnp.int32, (2 * owners, 2 * owners), 1)
         ).astype(f32)
-        weight_t = dot_t(eye, weight[...])
+        high, low = halves(dot_t(eye, weight[...]) * scaling)
+        weight_t = jnp.concatenate([high, high, low], axis=1)
         for copy in tables:
             copy.wait()
         cos, sin = twist[0], twist[1]
@@ -374,7 +399,8 @@
         def filter_phase():
             @pl.when(kind == 0)
             def _():
-                others(2 * wide, groups, trade)
+                others(3 * wide, groups, trade)
+                others(2 * wide, min(3 * wide, groups), trade)
 
                 @pl.when(2 * wide < groups)
                 def _():
@@ -398,7 +424,8 @@
                 ],
                 axis=1,
             )
-            filt = jnp.dot(weight_t, feats_all[...], precision=HIGHEST, preferred_element_type=f32) * scaling
+            high, low = halves(feats_all[...])
+            filt = dot(weight_t, jnp.concatenate([high, low, high], axis=0))
             send_filt[:, 0, :] = filt[:owners, :LANES]
             send_filt[:, 1, :] = filt[:owners, LANES:]
             send_filt[:, 2, :] = filt[owners:, :LANES]
@@ -440,16 +467,17 @@
             ],
             axis=0,
         )
-        part = dot_t(taps_here, feats_all[...])
+        feats_high, feats_low = halves(feats_all[...])
+        high, low = halves(taps_here)
+        part = rows_by_rows(high, feats_high) + rows_by_rows(low, feats_high) + rows_by_rows(high, feats_low)
         pairs = jnp.concatenate([part[:owners], part[owners:]], axis=1)
-        send_part[:, 0, :] = pairs[:reducers]
-        send_part[:, 1, :] = pairs[reducers:]
+        for n in range(4):
+            send_part[:, n, :] = pairs[n * reducers : (n + 1) * reducers]
 
         def push_part(k):
             @pl.when(jnp.logical_not(jnp.logical_and(reducer, k == my_reducer)))
             def _():
-                to = k // 2 * 4 + 1 + k % 2
-                push(send_part.at[k], recv_part.at[chip], 5, {"ctx": 2 * to + 1, "ch": group})
+                push(send_part.at[k], recv_part.at[chip], 5, {"ctx": 2 * reducer_chip(k) + 1, "ch": group})
 
         loop(0, reducers, push_part)
 
@@ -487,6 +515,22 @@
         far_first(1, shards, push_out)
         recv_out[pl.ds(chip, 1)] = send_out[pl.ds(me, 1)]
 
+        @pl.when(reducer)
+        def _():
+            arrived(recv_part, owners - 1, 5)
+            send_sum[pl.ds(0, 1)] = jnp.sum(recv_part[...], axis=0, keepdims=True) * (scaling * scaling)
+
+            def push_sum(k):
+                push(send_sum.at[0], recv_sum.at[my_reducer], 6, {"ctx": me ^ k, "ch": group})
+
+            far_first(1, shards, push_sum)
+            recv_sum[pl.ds(my_reducer, 1)] = send_sum[pl.ds(0, 1)]
+            sent(send_part, reducers - 1, 5)
+
+        @pl.when(jnp.logical_not(reducer))
+        def _():
+            sent(send_part, reducers, 5)
+
         def sent_odd(other):
             await_block(feat_sent, 1, other)
 
@@ -495,85 +539,78 @@
         sent(send_filt, owners - 1, 2)
         sent(send_taps, owners - 1, 3)
         sent(send_sig, owners - 1, 1)
-
-        @pl.when(reducer)
-        def _():
-            arrived(recv_part, owners - 1, 5)
-            send_sum[pl.ds(0, 1)] = jnp.sum(recv_part[...], axis=0, keepdims=True) * (scaling * scaling)
-
-            def push_sum(k):
-                push(send_sum.at[0], recv_sum.at[my_reducer], 6, {"ctx": me ^ k, "ch": group})
-
-            far_first(1, shards, push_sum)
-            recv_sum[pl.ds(my_reducer, 1)] = send_sum[pl.ds(0, 1)]
-            sent(send_part, reducers - 1, 5)
-
-        @pl.when(jnp.logical_not(reducer))
-        def _():
-            sent(send_part, reducers, 5)
-
         arrived(recv_out, owners - 1, 4)
         sent(send_out, shards - 1, 4)
 
     @pl.when(core == 0)
     def _():
+        await_block(feat_sent, 0, group)
+
+        @pl.when(jnp.logical_not(at_hub))
+        def _():
+            others(0, known, lambda other: await_block(feat_sent, 0, other))
+
+        sent(send_sig, owners, 1)
         arrived(recv_out, owners, 4)
-        await_block(feat_sent, 0, group)
-
-        @pl.when(jnp.logical_not(at_hub))
-        def _():
-            others(0, known, lambda other: await_block(feat_sent, 0, other))
-
-        sent(send_sig, owners, 1)
-
-    @pl.when(core == 1)
-    def _():
-        @pl.when(reducer)
-        def _():
-            arrived(recv_sum, reducers - 1, 6)
-            sent(send_sum, shards - 1, 6)
-
-        @pl.when(jnp.logical_not(reducer))
-        def _():
-            arrived(recv_sum, reducers, 6)
-
-    @pl.when(core == 0)
+
+    results = [
+        pltpu.make_async_copy(ref, target, out_sems.at[n])
+        for n, (ref, target) in enumerate(
+            [
+                (output, output_hbm),
+                (gate_grad, gate_grad_hbm),
+                (key_grad, key_grad_hbm),
+                (value_grad, value_grad_hbm),
+                (weight_grad, weight_grad_hbm),
+            ]
+        )
+    ]
+    conv = jnp.concatenate([recv_out[:, 0, :], recv_out[:, 1, :]], axis=0)
+    output[...] = (gate[...].astype(f32) * conv).astype(bf16)
+    results[0].start()
+    gate_grad[...] = (upstream[...].astype(f32) * conv).astype(bf16)
+    results[1].start()
+    mixed_grad = jnp.concatenate([recv_out[:, 2, :], recv_out[:, 3, :]], axis=0)
+    key_grad[...] = (mixed_grad * value[...].astype(f32)).astype(bf16)
+    results[2].start()
+    value_grad[...] = (mixed_grad * key[...].astype(f32)).astype(bf16)
+    results[3].start()
+
+    @pl.when(reducer)
+    def _():
+        arrived(recv_sum, reducers - 1, 6)
+
+    @pl.when(jnp.logical_not(reducer))
     def _():
         arrived(recv_sum, reducers, 6)
 
-
-def finish(*refs):
-    sources, targets = refs[:6], refs[6:11]
-    gate, key, value, upstream, out, total = refs[11:17]
-    results = refs[17:22]
-    in_sems, out_sems = refs[22:]
-    loads = [
-        pltpu.make_async_copy(source, ref, in_sems.at[n])
-        for n, (source, ref) in enumerate(zip(sources, (gate, key, value, upstream, out, total)))
-    ]
-    stores = [
-        pltpu.make_async_copy(ref, target, out_sems.at[n]) for n, (ref, target) in enumerate(zip(results, targets))
-    ]
-    for n in (4, 0, 3, 1, 2, 5):
-        loads[n].start()
-    loads[4].wait()
-    conv = jnp.concatenate([out[:, 0, :], out[:, 1, :]], axis=0)
-    mixed_grad = jnp.concatenate([out[:, 2, :], out[:, 3, :]], axis=0)
-    for n, (load, ref, factor) in enumerate(
-        [(0, gate, conv), (3, upstream, conv), (2, value, mixed_grad), (1, key, mixed_grad)]
-    ):
-        loads[load].wait()
-        results[n][...] = (ref[...].astype(f32) * factor).astype(bf16)
-        stores[n].start()
-    loads[5].wait()
-    sums = jnp.concatenate([total[:, 0, :], total[:, 1, :]], axis=0)
+    sums = jnp.concatenate([recv_sum[:, n, :] for n in range(4)], axis=0)
     half = sums.shape[1] // 2
-    grad_rows = jnp.concatenate([sums[:, :half], sums[:, half:]], axis=0)
     eye = (
         lax.broadcasted_iota(jnp.int32, (half, half), 0) == lax.broadcasted_iota(jnp.int32, (half, half), 1)
-    ).astype(f32)
-    results[4][...] = dot_t(eye, grad_rows)
-    stores[4].start()
+    ).astype(bf16)
+    high, low = halves(jnp.concatenate([sums[:, :half], sums[:, half:]], axis=0))
+    weight_grad[...] = rows_by_rows(eye, high) + rows_by_rows(eye, low)
+    results[4].start()
+
+    @pl.when(reducer)
+    def _():
+        sent(send_sum, shards - 1, 6)
+
+    for copy in results:
+        copy.wait()
+
+
+def hand_over(*refs):
+    sources, targets, held = refs[:5], refs[5:10], refs[10:15]
+    in_sems, out_sems = refs[15:]
+    loads = [pltpu.make_async_copy(source, ref, in_sems.at[n]) for n, (source, ref) in enumerate(zip(sources, held))]
+    stores = [pltpu.make_async_copy(ref, target, out_sems.at[n]) for n, (ref, target) in enumerate(zip(held, targets))]
+    for load in loads:
+        load.start()
+    for load, store in zip(loads, stores):
+        load.wait()
+        store.start()
     for store in stores:
         store.wait()
 
@@ -583,23 +620,24 @@
     channels, length = gate_input.shape
     feat = filter_weight.shape[0]
     owners = shards // 2
-    reducers = owners // 2
+    reducers = owners // 4
     assert channels == 2 * owners and length == LANES and feat == LANES // 2
     tables = make_tables(shards)
     hbm = pl.BlockSpec(memory_space=pl.ANY)
-    vmem = pl.BlockSpec(memory_space=pltpu.VMEM)
     rows = lambda count, width: pltpu.VMEM((count, width, LANES), f32)
     block = jax.ShapeDtypeStruct((channels, length), bf16)
     per = features.shape[0]
-    out, total = pl.pallas_call(
+    shapes = (block, block, block, block, jax.ShapeDtypeStruct((feat, channels), f32))
+    results = pl.pallas_call(
         functools.partial(kernel, shards, groups),
-        out_shape=(
-            jax.ShapeDtypeStruct((owners, 4, LANES), f32),
-            jax.ShapeDtypeStruct((reducers, 2, LANES), f32),
-        ),
+        out_shape=shapes,
         in_specs=[hbm] * 10,
-        out_specs=(vmem,) * 2,
+        out_specs=(hbm,) * 5,
         scratch_shapes=[
+            *[pltpu.VMEM((channels, length), bf16)] * 4,
+            pltpu.VMEM((feat, channels), f32),
+            rows(owners, 4),
+            rows(reducers, 4),
             *[pltpu.VMEM((channels, length), bf16)] * 4,
             pltpu.VMEM(filter_weight.shape, f32),
             *[pltpu.VMEM(table.shape, f32) for table in tables],
@@ -614,10 +652,11 @@
             rows(owners, 4),
             rows(owners, 4),
             rows(owners, 4),
-            rows(reducers, 2),
-            rows(owners, 2),
-            rows(shards, 2),
+            rows(reducers, 4),
+            rows(owners, 4),
             rows(shards, 4),
+            rows(shards, 4),
+            pltpu.SemaphoreType.DMA((5,)),
             pltpu.SemaphoreType.DMA((5,)),
             pltpu.SemaphoreType.DMA((4,)),
             pltpu.SemaphoreType.DMA,
@@ -634,21 +673,18 @@
         ),
     )(gate_input, key_input, value_input, features, filter_weight, out_grad, *tables)
     return pl.pallas_call(
-        finish,
-        out_shape=(block, block, block, block, jax.ShapeDtypeStruct((feat, channels), f32)),
-        in_specs=[hbm] * 6,
+        hand_over,
+        out_shape=shapes,
+        in_specs=[hbm] * 5,
         out_specs=(hbm,) * 5,
         scratch_shapes=[
             *[pltpu.VMEM((channels, length), bf16)] * 4,
-            rows(owners, 4),
-            rows(reducers, 2),
-            *[pltpu.VMEM((channels, length), bf16)] * 4,
             pltpu.VMEM((feat, channels), f32),
-            pltpu.SemaphoreType.DMA((6,)),
+            pltpu.SemaphoreType.DMA((5,)),
             pltpu.SemaphoreType.DMA((5,)),
         ],
         compiler_params=pltpu.CompilerParams(vmem_limit_bytes=56 * 1024 * 1024),
-    )(gate_input, key_input, value_input, out_grad, out, total)
+    )(*results)
 
 
 def solution(mesh):

time: 42.4 us -> 41.9 us (0.988)
  Pallas kernels: 41.5 us -> 40.9 us
    pallas_call x2, Pallas kernels: 41.5 us -> 40.9 us  [the longest x1 39.4 us: on_device(): pl.pallas_call(functools.partial(kernel, shards, groups), out_shape=shape...]
where the time goes in v4:
time: 41.9 us; the launch traced here: 41.6 us
  Pallas kernels  40.9 us (98%)
  between operations  0.64 us (2%)
    pallas_call x1, Pallas kernels, on_device(): pl.pallas_call(functools.partial(kernel, shards, groups), out_shape=shape...  39.4 us
    pallas_call x1, Pallas kernels, on_device(): pl.pallas_call(hand_over, out_shape=shapes, in_specs=[hbm] * 5, out_specs...  1.53 us

profile of v4, /device:TPU:1, one launch (start us, length us, event | category | flops | bytes accessed | tf_op | source)
XLA Modules:
  0.0 41.6 jit_solution(8967053363002673597)
XLA Ops:
  0.6 39.4 %shard_map.137 = (bf16[64,128]{1,0:T(8,128)(2,1)}, bf16[64,128]{1,0:T(8,128)(2,1)}, bf16[64,128]{1,0:T(8,128)(2,1)}, bf16[64,128]{1,0:T(8,128)(2,1)}, f32[64,64]{1,0:T(8,128)}) custom-call(bf16[64,128]{1,0:T(8,128)(2,1)} %gate_in.1, bf16[64,128]{1,0:T(8,128)(2,1)} %key_in.1, bf16[64,128]{1,0:T(8,128)(2,1)} %value_in.1, f32[4,128]{1,0:T(4,128)} %feats_in.1, ...), custom_call_target="tpu_custom_call" | custom-call | tf_op jit(solution)/shard_map/pallas_call | solution.py:631
  40.0 1.5 %shard_map.138 = (bf16[64,128]{1,0:T(8,128)(2,1)}, bf16[64,128]{1,0:T(8,128)(2,1)}, bf16[64,128]{1,0:T(8,128)(2,1)}, bf16[64,128]{1,0:T(8,128)(2,1)}, f32[64,64]{1,0:T(8,128)}) custom-call(bf16[64,128]{1,0:T(8,128)(2,1)} %get-tuple-element.10.refs_0_, bf16[64,128]{1,0:T(8,128)(2,1)} %get-tuple-element.11.refs_1_, bf16[64,128]{1,0:T(8,128)(2,1)} %get-tuple-element.12.refs_2_, ...), custom_call_target="tpu_custom_call" | custom-call | tf_op jit(solution)/shard_map/pallas_call | solution.py:675

commit v5 on v4

--- a/solution.py
+++ b/solution.py
@@ -76,13 +76,13 @@
             jnp.concatenate([along * cos - across * sin, -(across * cos + along * sin)], axis=1)
         )
     high, low = halves(jnp.concatenate(turned, axis=0))
-    return dot(high, mid[0]) + dot(low, mid[0]) + dot(high, mid[1])
+    return dot(jnp.concatenate([high, low, high], axis=1), mid[...])
 
 
 def signals_of(products, last, mid, cos, sin):
     rows = cos.shape[0]
     high, low = halves(jnp.concatenate(products, axis=0))
-    inner = dot(high, mid[0]) + dot(low, mid[0]) + dot(high, mid[1])
+    inner = dot(jnp.concatenate([high, low, high], axis=1), mid[...])
     turned = []
     for index in range(len(products)):
         part = inner[index * rows : (index + 1) * rows]
@@ -369,8 +369,9 @@
             high, low = halves(first[n])
             first_split[n] = jnp.concatenate([high, high, low], axis=1)
             last_split[2 * n], last_split[2 * n + 1] = halves(last[n])
-            mid_split[2 * n], mid_split[2 * n + 1] = halves(mid[n])
-        forward, backward = (mid_split[0], mid_split[1]), (mid_split[2], mid_split[3])
+            high, low = halves(mid[n])
+            mid_split[n] = jnp.concatenate([high, high, low], axis=0)
+        forward, backward = mid_split.at[0], mid_split.at[1]
         lasts = [(last_split[0], last_split[1]), (last_split[2], last_split[3])]
 
         own_feats.wait()
@@ -400,7 +401,7 @@
             @pl.when(kind == 0)
             def _():
                 others(3 * wide, groups, trade)
-                others(2 * wide, min(3 * wide, groups), trade)
+                others(2 * wide, min(3 * wide, groups), await_feats)
 
                 @pl.when(2 * wide < groups)
                 def _():
@@ -432,6 +433,10 @@
             send_filt[:, 3, :] = filt[owners:, LANES:]
             far_first(1, owners, push_filt)
             recv_filt[pl.ds(chip, 1)] = send_filt[pl.ds(chip, 1)]
+
+            @pl.when(kind == 0)
+            def _():
+                others(2 * wide, min(3 * wide, groups), push_both)
 
         @pl.when(kind == 0)
         def _():
@@ -643,7 +648,7 @@
             *[pltpu.VMEM(table.shape, f32) for table in tables],
             pltpu.VMEM((2, tables[0].shape[1], 3 * tables[0].shape[2]), bf16),
             pltpu.VMEM((4, *tables[1].shape[1:]), bf16),
-            pltpu.VMEM((4, *tables[2].shape[1:]), bf16),
+            pltpu.VMEM((2, 3 * tables[2].shape[1], tables[2].shape[2]), bf16),
             rows(2 * groups, per),
             pltpu.VMEM((feat, 2 * LANES), f32),
             rows(owners, 4),

time: 41.9 us -> 41.9 us (level)
  no operation moved by 1% of the time
where the time goes in v5:
time: 41.9 us; the launch traced here: 41.6 us
  Pallas kernels  40.9 us (98%)
  between operations  0.64 us (2%)
    pallas_call x1, Pallas kernels, on_device(): pl.pallas_call(functools.partial(kernel, shards, groups), out_shape=shape...  39.4 us
    pallas_call x1, Pallas kernels, on_device(): pl.pallas_call(hand_over, out_shape=shapes, in_specs=[hbm] * 5, out_specs...  1.53 us

profile of v5, /device:TPU:1, one launch (start us, length us, event | category | flops | bytes accessed | tf_op | source)
XLA Modules:
  0.0 41.6 jit_solution(12950193208455558752)
XLA Ops:
  0.6 39.4 %shard_map.137 = (bf16[64,128]{1,0:T(8,128)(2,1)}, bf16[64,128]{1,0:T(8,128)(2,1)}, bf16[64,128]{1,0:T(8,128)(2,1)}, bf16[64,128]{1,0:T(8,128)(2,1)}, f32[64,64]{1,0:T(8,128)}) custom-call(bf16[64,128]{1,0:T(8,128)(2,1)} %gate_in.1, bf16[64,128]{1,0:T(8,128)(2,1)} %key_in.1, bf16[64,128]{1,0:T(8,128)(2,1)} %value_in.1, f32[4,128]{1,0:T(4,128)} %feats_in.1, ...), custom_call_target="tpu_custom_call" | custom-call | tf_op jit(solution)/shard_map/pallas_call | solution.py:636
  40.0 1.5 %shard_map.138 = (bf16[64,128]{1,0:T(8,128)(2,1)}, bf16[64,128]{1,0:T(8,128)(2,1)}, bf16[64,128]{1,0:T(8,128)(2,1)}, bf16[64,128]{1,0:T(8,128)(2,1)}, f32[64,64]{1,0:T(8,128)}) custom-call(bf16[64,128]{1,0:T(8,128)(2,1)} %get-tuple-element.10.refs_0_, bf16[64,128]{1,0:T(8,128)(2,1)} %get-tuple-element.11.refs_1_, bf16[64,128]{1,0:T(8,128)(2,1)} %get-tuple-element.12.refs_2_, ...), custom_call_target="tpu_custom_call" | custom-call | tf_op jit(solution)/shard_map/pallas_call | solution.py:680
